TPU v7x, 512 devices: a whole 4x8x8 slice. The times are simulated.
512 devices in a mesh: dp: 8 (over z_lo, core), expert: 64 (over x, z_hi, y).
Axes of the slice: x: 4, y: 8, z: 8 (z_hi: 2, z_lo: 4; z = z_hi * 4 + z_lo), core: 2. Of those that a mesh axis runs over, the one named last changes fastest.
Arguments:
- tokens: bfloat16 [12288, 4096], P('expert', 'dp'), may hold values from -6 to 6
- cotangent: bfloat16 [12288, 4096], P('expert', 'dp'), may hold values from -6 to 6
- gate_scale: float32 [12288, 2], P('expert'), may hold values from 0.1 to 1
- expert_ids: int32 [12288, 2], P('expert'), may hold values from 0 to 47, as said below
- expert_slots: int32 [48, 2], replicated, may hold values from 0 to 63, as said below
- hot_pairs: int32 [16], replicated, may hold values from 0 to 31, as said below
- w_gate: bfloat16 [64, 4096, 1024], P('expert', 'dp'), as said below
- w_up: bfloat16 [64, 4096, 1024], P('expert', 'dp'), as said below
- w_down: bfloat16 [64, 1024, 4096], P('expert', None, 'dp'), as said below
Outputs:
- grad_tokens: bfloat16 [12288, 4096], P('expert', 'dp')
- grad_down: bfloat16 [64, 1024, 4096], P('expert', None, 'dp')
Inputs may be any that keep to these rules, and one draw needn't show every extreme that they name: `expert_ids`: route k of every token names an expert whose slots have parity k. With the slot expert_slots[e, t mod 2], at most 12 routes of the tokens of one index of expert go to one slot, and in every draw some slot receives exactly 12 routes from every index. `expert_slots`: every slot belongs to exactly one expert. Both entries of a row are equal unless the expert is hot; then the second is the first plus 64 / 2. `hot_pairs`: Distinct, in no particular order; exactly the first slots of the hot experts; as many even as odd; 0 and 31 are always among them. `w_gate`: the two slots of a hot expert hold equal weights. `w_up`: the two slots of a hot expert hold equal weights. `w_down`: the two slots of a hot expert hold equal weights.
All inputs are finite; a program needn't handle non-finite values.
Results may differ from a plain program's by a relative error of at most 0.029.
Values may be sent and summed in bfloat16 or wider, within the bound.
A program may use at most 64 MiB of HBM per device.

v0:
```python
import jax
import jax.numpy as jnp
from jax import lax
from jax.sharding import PartitionSpec as P


def from_partner(block, axis, stride):
    count = lax.axis_size(axis)
    route = []
    for low in range(count):
        high = low | 1 << stride
        if high != low and high < count:
            route += [(low, high), (high, low)]
    return lax.ppermute(block, axis, route)


def swiglu_back(gate_sum, up_sum, grad_hidden):
    sigmoid_gate = jax.nn.sigmoid(gate_sum)
    active = gate_sum * sigmoid_gate
    hidden = (active * up_sum).astype(jnp.bfloat16)
    grad_up = (grad_hidden * active).astype(jnp.bfloat16)
    grad_gate = (
        grad_hidden * up_sum * sigmoid_gate * (1.0 + gate_sum * (1.0 - sigmoid_gate))
    ).astype(jnp.bfloat16)
    return (hidden, grad_gate, grad_up)


def contract_last(left, right):
    return lax.dot_general(
        left, right, (((1,), (1,)), ((), ())), preferred_element_type=jnp.float32
    )


def contract_first(left, right):
    return lax.dot_general(
        left, right, (((0,), (0,)), ((), ())), preferred_element_type=jnp.float32
    )


def on_device(
    tokens, cotangent, gate_scale, expert_ids, expert_slots, hot_pairs, w_gate, w_up, w_down
):
    tok_rows, width = tokens.shape
    route_count = expert_ids.shape[1]
    slot_count = lax.axis_size("expert")
    capacity = 2 * tok_rows * route_count // slot_count
    entries = tok_rows * route_count
    expert_iota = jnp.arange(expert_slots.shape[0], dtype=jnp.int32)
    expert_match = expert_ids[:, :, None] == expert_iota
    parity = (jnp.arange(tok_rows, dtype=jnp.int32) % 2)[:, None, None]
    slot_table = jnp.where(parity == 1, expert_slots[:, 1], expert_slots[:, 0])
    route_slot = jnp.sum(jnp.where(expert_match, slot_table, 0), axis=2).reshape(entries)
    slot_hit = (route_slot[:, None] == jnp.arange(slot_count, dtype=jnp.int32)).astype(jnp.int32)
    before = jnp.cumsum(slot_hit, axis=0) - slot_hit
    target = route_slot * capacity + jnp.sum(before * slot_hit, axis=1)
    placing = (
        jnp.arange(slot_count * capacity, dtype=jnp.int32)[:, None] == target[None, :]
    ).astype(jnp.bfloat16)
    repeated = jnp.broadcast_to(tokens[:, None, :], (tok_rows, route_count, width)).reshape(
        entries, width
    )
    scaled = (
        (gate_scale[:, :, None] * cotangent[:, None, :].astype(jnp.float32))
        .astype(jnp.bfloat16)
        .reshape(entries, width)
    )
    send_x = (
        jnp.dot(placing, repeated, preferred_element_type=jnp.float32)
        .astype(jnp.bfloat16)
        .reshape(slot_count, capacity, width)
    )
    send_dy = (
        jnp.dot(placing, scaled, preferred_element_type=jnp.float32)
        .astype(jnp.bfloat16)
        .reshape(slot_count, capacity, width)
    )
    recv_x, recv_dy = (
        lax.all_to_all(send_x, "expert", split_axis=0, concat_axis=0, tiled=True),
        lax.all_to_all(send_dy, "expert", split_axis=0, concat_axis=0, tiled=True),
    )
    rows_x = recv_x.reshape(-1, width)
    rows_dy = recv_dy.reshape(-1, width)
    gate_weight = w_gate[0]
    up_weight = w_up[0]
    down_weight = w_down[0]
    gate_part = jnp.dot(rows_x, gate_weight, preferred_element_type=jnp.float32)
    up_part = jnp.dot(rows_x, up_weight, preferred_element_type=jnp.float32)
    hidden_part = contract_last(rows_dy, down_weight)
    gate_part, up_part, hidden_part = (gate_part, up_part, hidden_part)
    gate_sum, up_sum, grad_hidden = (
        lax.psum(gate_part.astype(jnp.bfloat16), "dp").astype(jnp.float32),
        lax.psum(up_part.astype(jnp.bfloat16), "dp").astype(jnp.float32),
        lax.psum(hidden_part.astype(jnp.bfloat16), "dp").astype(jnp.float32),
    )
    hidden, grad_gate, grad_up = swiglu_back(gate_sum, up_sum, grad_hidden)
    route_grad = (contract_last(grad_gate, gate_weight) + contract_last(grad_up, up_weight)).astype(
        jnp.bfloat16
    )
    returned = lax.all_to_all(
        route_grad.reshape(slot_count, capacity, width),
        "expert",
        split_axis=0,
        concat_axis=0,
        tiled=True,
    )
    per_route = contract_first(placing, returned.reshape(-1, width))
    grad_tokens = jnp.sum(per_route.reshape(tok_rows, route_count, width), axis=1).astype(
        jnp.bfloat16
    )
    own_grad = contract_first(hidden, rows_dy)
    pair_bit = slot_count.bit_length() - 2
    half_slots = slot_count // 2
    hot_flag = jnp.any(hot_pairs == lax.axis_index("expert") % half_slots).astype(jnp.float32)
    partner = from_partner(own_grad.astype(jnp.bfloat16), "expert", pair_bit).astype(own_grad.dtype)
    grad_down = (own_grad + hot_flag * partner).astype(jnp.bfloat16)[None]
    return (grad_tokens, grad_down)


def solution(mesh):
    placed = (
        P("expert", "dp"),
        P("expert", "dp"),
        P("expert", None),
        P("expert", None),
        P(),
        P(),
        P("expert", "dp", None),
        P("expert", "dp", None),
        P("expert", None, "dp"),
    )
    return jax.shard_map(
        on_device,
        mesh=mesh,
        in_specs=placed,
        out_specs=(P("expert", "dp"), P("expert", None, "dp")),
        check_vma=False,
    )
```

profile of v0, /device:TPU:1, one launch (start us, length us, event | category | flops | bytes accessed | tf_op | source)
XLA Modules:
  0.0 303.0 jit_solution(2271544175726176611)
XLA Ops:
  7.2 0.0 copy-start
  7.2 0.8 slice_bitcast_fusion.1
  8.0 0.1 broadcast_select_fusion
  8.1 0.7 select_reduce_fusion
  8.8 0.1 copy.16
  8.9 0.1 eq.91
  9.0 0.1 reshape.141
  9.2 0.9 reduce-window.6
  10.1 0.2 slice_reduce_fusion
  10.4 0.1 fusion.29
  10.5 1.1 broadcast_in_dim.56
  11.6 0.2 reshape.145
  11.8 0.6 convolution_convert_fusion.3
  12.4 0.0 copy-start.4
  12.4 1.1 reshape.146
  13.5 0.0 copy-start.5
  13.5 19.7 %all-to-all-start.1 = ((bf16[64,12,512]{2,1,0:T(8,128)(2,1)}), bf16[64,12,512]{2,1,0:T(8,128)(2,1)S(1)}, u32[]{:S(2)}, u32[]{:S(2)}) async-start(bf16[64,12,512]{2,1,0:T(8,128)(2,1)} %reshape.146), calls=%async_computation.1 | async-start | bytes 2097152 | tf_op jit(solution)/shard_map/all_to_all | solution.py:78
  33.3 0.0 copy-done.4
  33.3 0.2 mul.63
  33.5 1.4 mul.64
  34.9 0.0 copy-done.5
  34.9 0.1 copy.19
  35.0 0.1 mul.61
  35.2 1.8 convolution_convert_fusion.4
  37.0 1.1 reshape.143
  38.1 25.2 %all-to-all-done.1 = bf16[64,12,512]{2,1,0:T(8,128)(2,1)S(1)} async-done(((bf16[64,12,512]{2,1,0:T(8,128)(2,1)}), bf16[64,12,512]{2,1,0:T(8,128)(2,1)S(1)}, u32[]{:S(2)}, u32[]{:S(2)}) %all-to-all-start.1) | async-done | bytes 786464 | tf_op jit(solution)/shard_map/all_to_all | solution.py:78
  63.3 8.0 %all-to-all-start = ((bf16[64,12,512]{2,1,0:T(8,128)(2,1)}), bf16[64,12,512]{2,1,0:T(8,128)(2,1)S(1)}, u32[]{:S(2)}, u32[]{:S(2)}) async-start(bf16[64,12,512]{2,1,0:T(8,128)(2,1)} %reshape.143), calls=%async_computation | async-start | bytes 2097152 | tf_op jit(solution)/shard_map/all_to_all | solution.py:79
  71.3 0.0 all-reduce.3.cloned.1.call-start
  71.4 1.1 reshape.147
  72.4 0.0 copy-done
  72.4 0.0 copy-start.3
  72.4 0.0 copy-start.8
  72.4 3.4 %convolution_convert_fusion = bf16[768,1024]{1,0:T(8,128)(2,1)} fusion(bf16[768,512]{1,0:T(8,128)(2,1)} %reshape.147, bf16[1,512,1024]{2,1,0:T(8,128)(2,1)S(1)} %copy-done), kind=kOutput, calls=%fused_computation.16 | convolution fusion | flops 806092800 | bytes 3407872 | tf_op jit(solution)/shard_map/dot_general | solution.py:86
  75.8 0.0 copy-done.3
  75.8 0.0 copy-done.8
  75.8 2.1 convolution_convert_fusion.1
  78.0 21.6 %all-to-all-done = bf16[64,12,512]{2,1,0:T(8,128)(2,1)S(1)} async-done(((bf16[64,12,512]{2,1,0:T(8,128)(2,1)}), bf16[64,12,512]{2,1,0:T(8,128)(2,1)S(1)}, u32[]{:S(2)}, u32[]{:S(2)}) %all-to-all-start) | async-done | bytes 786464 | tf_op jit(solution)/shard_map/all_to_all | solution.py:79
  99.5 0.2 reshape.144
  99.7 0.0 copy-start.1
  99.7 3.7 %convolution_convert_fusion.2 = bf16[768,1024]{1,0:T(8,128)(2,1)} fusion(bf16[768,512]{1,0:T(8,128)(2,1)S(1)} %reshape.144, bf16[1,1024,512]{2,1,0:T(8,128)(2,1)} %param.17), kind=kOutput, calls=%fused_computation.18 | convolution fusion | flops 806092800 | bytes 3407872 | tf_op jit(solution)/shard_map/dot_general | solution.py:29
  103.4 0.0 copy-done.1
  103.4 0.0 all-reduce.3.cloned.1.call-update
  103.5 123.5 %all-reduce.3.cloned.1.call-done = (bf16[768,1024]{1,0:T(8,128)(2,1)}, bf16[768,1024]{1,0:T(8,128)(2,1)}, bf16[768,1024]{1,0:T(8,128)(2,1)}) async-done(((bf16[768,1024]{1,0:T(8,128)(2,1)}, bf16[768,1024]{1,0:T(8,128)(2,1)}, bf16[768,1024]{1,0:T(8,128)(2,1)}), (bf16[768,1024]{1,0:T(8,128)(2,1)}, bf16[768,1024]{1,0:T(8,128)(2,1)}, bf16[768,1024]{1,0:T(8,128)(2,1)})) %all-reduce.3.cloned.1.call-update) | async-done | bytes 4718608 | tf_op jit(solution)/shard_map/psum | solution.py:92
  227.0 0.0 copy-start.6
  227.0 4.1 %fusion.13 = f32[768,512]{1,0:T(8,128)S(1)} fusion(bf16[768,1024]{1,0:T(8,128)(2,1)} %get-tuple-element.2, bf16[768,1024]{1,0:T(8,128)(2,1)} %get-tuple-element.3, bf16[768,1024]{1,0:T(8,128)(2,1)} %get-tuple-element.4, bf16[1,512,1024]{2,1,0:T(8,128)(2,1)S(1)} %copy-done), kind=kOutput, calls=%fused_computation.22 | convolution fusion | flops 815529984 | bytes 7340032 | tf_op jit(solution)/shard_map/dot_general | solution.py:29
  231.1 0.0 copy-done.6
  231.1 0.0 copy-done.7
  231.1 0.0 copy-done.9
  231.1 1.2 add_convert_fusion.1
  232.3 1.2 reshape.148
  233.4 15.1 %all-to-all-start.2 = ((bf16[64,12,512]{2,1,0:T(8,128)(2,1)}), bf16[64,12,512]{2,1,0:T(8,128)(2,1)S(1)}, u32[]{:S(2)}, u32[]{:S(2)}) async-start(bf16[64,12,512]{2,1,0:T(8,128)(2,1)} %reshape.148), calls=%async_computation.2 | async-start | bytes 2097152 | tf_op jit(solution)/shard_map/all_to_all | solution.py:99
  248.6 0.0 copy-done.2
  248.6 0.0 copy-start.10
  248.6 4.8 %fusion.35 = (bf16[1024,512]{1,0:T(8,128)(2,1)}, f32[1024,512]{1,0:T(8,128)}) fusion(bf16[768,512]{1,0:T(8,128)(2,1)S(1)} %copy-done.2, bf16[768,1024]{1,0:T(8,128)(2,1)} %get-tuple-element.2, bf16[768,1024]{1,0:T(8,128)(2,1)} %get-tuple-element.4), kind=kOutput, calls=%fused_computation.60 | convolution fusion | flops 812122112 | bytes 7077888 | tf_op jit(solution)/shard_map/dot_general | solution.py:35
  253.4 4.5 %collective-permute-start = (bf16[1024,512]{1,0:T(8,128)(2,1)}, bf16[1024,512]{1,0:T(8,128)(2,1)S(1)}, u32[]{:S(2)}, u32[]{:S(2)}) collective-permute-start(bf16[1024,512]{1,0:T(8,128)(2,1)} %get-tuple-element.7), channel_id=1, source_target_pairs={{0,32},{32,0},{1,33},{33,1},{2,34},{34,2},{3,35},{35,3},{4,36},{36... | collective-permute-start | bytes 3145736 | tf_op jit(solution)/shard_map/ppermute | solution.py:14
  257.9 0.0 copy-done.10
  257.9 0.6 compare_reduce_fusion
  259.2 0.2 iota_compare_fusion.3
  259.5 1.1 eq.97
  260.6 30.2 %collective-permute-done = bf16[1024,512]{1,0:T(8,128)(2,1)S(1)} collective-permute-done((bf16[1024,512]{1,0:T(8,128)(2,1)}, bf16[1024,512]{1,0:T(8,128)(2,1)S(1)}, u32[]{:S(2)}, u32[]{:S(2)}) %collective-permute-start) | collective-permute-done | bytes 1048608 | tf_op jit(solution)/shard_map/ppermute | solution.py:14
  290.8 2.9 fusion.18
  293.7 0.0 all-to-all-done.2
  293.7 0.2 reshape.150
  293.9 2.3 convolution_reduce_fusion
  (7 shorter events, 0.1 us)
Async XLA Ops:
  7.2 65.2 %copy-start = (bf16[1,512,1024]{2,1,0:T(8,128)(2,1)S(1)}, bf16[1,512,1024]{2,1,0:T(8,128)(2,1)}, u32[]{:S(2)}) copy-start(bf16[1,512,1024]{2,1,0:T(8,128)(2,1)} %param.15) | copy-start | bytes 3145732
  12.4 20.9 %copy-start.4 = (bf16[192,512]{1,0:T(8,128)(2,1)S(1)}, bf16[192,512]{1,0:T(8,128)(2,1)}, u32[]{:S(2)}) copy-start(bf16[192,512]{1,0:T(8,128)(2,1)} %param.10) | copy-start | bytes 589828
  13.5 21.4 %copy-start.5 = (f32[192,2]{0,1:T(2,128)S(1)}, f32[192,2]{0,1:T(2,128)}, u32[]{:S(2)}) copy-start(f32[192,2]{0,1:T(2,128)} %param.11) | copy-start | bytes 4612
  13.5 49.8 %all-to-all-start.1 = ((bf16[64,12,512]{2,1,0:T(8,128)(2,1)}), bf16[64,12,512]{2,1,0:T(8,128)(2,1)S(1)}, u32[]{:S(2)}, u32[]{:S(2)}) async-start(bf16[64,12,512]{2,1,0:T(8,128)(2,1)} %reshape.146), calls=%async_computation.1 | async-start | bytes 2097152 | tf_op jit(solution)/shard_map/all_to_all | solution.py:78
  63.3 36.2 %all-to-all-start = ((bf16[64,12,512]{2,1,0:T(8,128)(2,1)}), bf16[64,12,512]{2,1,0:T(8,128)(2,1)S(1)}, u32[]{:S(2)}, u32[]{:S(2)}) async-start(bf16[64,12,512]{2,1,0:T(8,128)(2,1)} %reshape.143), calls=%async_computation | async-start | bytes 2097152 | tf_op jit(solution)/shard_map/all_to_all | solution.py:79
  71.3 155.7 %all-reduce.3.cloned.1.call-start = ((), (), s32[]{:S(2)}) async-start(), calls=%async_computation.3 | async-start | bytes 9437184 | tf_op jit(solution)/shard_map/psum | solution.py:92
  72.4 3.4 %copy-start.3 = (bf16[768,512]{1,0:T(8,128)(2,1)S(1)}, bf16[768,512]{1,0:T(8,128)(2,1)}, u32[]{:S(2)}) copy-start(bf16[768,512]{1,0:T(8,128)(2,1)} %reshape.147) | copy-start | bytes 2359300
  72.4 3.4 %copy-start.8 = (bf16[1,512,1024]{2,1,0:T(8,128)(2,1)S(1)}, bf16[1,512,1024]{2,1,0:T(8,128)(2,1)}, u32[]{:S(2)}) copy-start(bf16[1,512,1024]{2,1,0:T(8,128)(2,1)} %param.16) | copy-start | bytes 3145732
  99.7 3.8 %copy-start.1 = (bf16[768,512]{1,0:T(8,128)(2,1)}, bf16[768,512]{1,0:T(8,128)(2,1)S(1)}, u32[]{:S(2)}) copy-start(bf16[768,512]{1,0:T(8,128)(2,1)S(1)} %reshape.144) | copy-start | bytes 2359300
  227.0 4.1 %copy-start.6 = (bf16[768,1024]{1,0:T(8,128)(2,1)S(1)}, bf16[768,1024]{1,0:T(8,128)(2,1)}, u32[]{:S(2)}) copy-start(bf16[768,1024]{1,0:T(8,128)(2,1)} %get-tuple-element.4) | copy-start | bytes 4718596
  227.0 4.1 %copy-start.7 = (bf16[768,1024]{1,0:T(8,128)(2,1)S(1)}, bf16[768,1024]{1,0:T(8,128)(2,1)}, u32[]{:S(2)}) copy-start(bf16[768,1024]{1,0:T(8,128)(2,1)} %get-tuple-element.3) | copy-start | bytes 4718596
  227.0 4.1 %copy-start.9 = (bf16[1,512,1024]{2,1,0:T(8,128)(2,1)S(1)}, bf16[1,512,1024]{2,1,0:T(8,128)(2,1)}, u32[]{:S(2)}) copy-start(bf16[1,512,1024]{2,1,0:T(8,128)(2,1)} %param.16) | copy-start | bytes 3145732
  232.3 16.3 %copy-start.2 = (bf16[768,512]{1,0:T(8,128)(2,1)S(1)}, bf16[768,512]{1,0:T(8,128)(2,1)}, u32[]{:S(2)}) copy-start(bf16[768,512]{1,0:T(8,128)(2,1)} %copy-done.1) | copy-start | bytes 2359300
  233.4 60.3 %all-to-all-start.2 = ((bf16[64,12,512]{2,1,0:T(8,128)(2,1)}), bf16[64,12,512]{2,1,0:T(8,128)(2,1)S(1)}, u32[]{:S(2)}, u32[]{:S(2)}) async-start(bf16[64,12,512]{2,1,0:T(8,128)(2,1)} %reshape.148), calls=%async_computation.2 | async-start | bytes 2097152 | tf_op jit(solution)/shard_map/all_to_all | solution.py:99
  248.6 9.3 %copy-start.10 = (s32[16]{0:T(128)S(1)}, s32[16]{0:T(128)}, u32[]{:S(2)}) copy-start(s32[16]{0:T(128)} %param.14) | copy-start | bytes 196
  253.4 37.4 %collective-permute-start = (bf16[1024,512]{1,0:T(8,128)(2,1)}, bf16[1024,512]{1,0:T(8,128)(2,1)S(1)}, u32[]{:S(2)}, u32[]{:S(2)}) collective-permute-start(bf16[1024,512]{1,0:T(8,128)(2,1)} %get-tuple-element.7), channel_id=1, source_target_pairs={{0,32},{32,0},{1,33},{33,1},{2,34},{34,2},{3,35},{35,3},{4,36},{36... | collective-permute-start | bytes 3145736 | tf_op jit(solution)/shard_map/ppermute | solution.py:14
Sparse Core Ops, SparseCore 0:
  103.6 123.3 all-reduce.2
where the time goes:
time: 304 us; the launch traced here: 303 us
  waiting for transfers between devices  201 us (66%)
  starting transfers between devices  47.4 us (16%)
  matrix products  24 us (8%)
  between operations  14.9 us (5%)
  local copies, waits for them, and re-layouts  10.6 us (3%)
  other arithmetic  5.66 us (2%)
    psum x1, waiting for transfers between devices, on_device(): lax.psum(up_part.astype(jnp.bfloat16), 'dp').astype(jnp.float32)  124 us
    ppermute x1, waiting for transfers between devices, from_partner(): return lax.ppermute(block, axis, route)  30.2 us
    all_to_all x1, waiting for transfers between devices, on_device(): lax.all_to_all(send_x, 'expert', split_axis=0, concat_axis=0, tiled=True)  25.2 us
    all_to_all x1, waiting for transfers between devices, on_device(): lax.all_to_all(send_dy, 'expert', split_axis=0, concat_axis=0, tiled=True)  21.6 us
    all_to_all x1, starting transfers between devices, on_device(): lax.all_to_all(send_x, 'expert', split_axis=0, concat_axis=0, tiled=True)  19.7 us
    all_to_all x1, starting transfers between devices, on_device(): lax.all_to_all(route_grad.reshape(slot_count, capacity, width), 'expert',...  15.1 us
    dot_general x3, matrix products, contract_last(): lax.dot_general(left, right, (((1,), (1,)), ((), ())), preferred_element_...  9.02 us
    all_to_all x1, starting transfers between devices, on_device(): lax.all_to_all(send_dy, 'expert', split_axis=0, concat_axis=0, tiled=True)  7.98 us
  transfers between devices with their start and end apart: 5, of which 4 were waited for; matrix products, arithmetic and copies ran while one was open for 7% of the time, Pallas kernels for 0%

commit v1 on v0

--- a/solution.py
+++ b/solution.py
@@ -1,7 +1,267 @@
 import jax
 import jax.numpy as jnp
 from jax import lax
+from jax.experimental import pallas as pl
+from jax.experimental.pallas import tpu as pltpu
 from jax.sharding import PartitionSpec as P
+
+BF = jnp.bfloat16
+F32 = jnp.float32
+MESH = pl.DeviceIdType.MESH
+CHUNK = 32
+
+
+def swiglu_back(gate_sum, up_sum, grad_hidden):
+    sigmoid_gate = jax.nn.sigmoid(gate_sum)
+    active = gate_sum * sigmoid_gate
+    hidden = (active * up_sum).astype(BF)
+    grad_up = (grad_hidden * active).astype(BF)
+    grad_gate = (
+        grad_hidden * up_sum * sigmoid_gate * (1.0 + gate_sum * (1.0 - sigmoid_gate))
+    ).astype(BF)
+    return (hidden, grad_gate, grad_up)
+
+
+def dot_last(left, right):
+    return lax.dot_general(left, right, (((1,), (1,)), ((), ())), preferred_element_type=F32)
+
+
+def dot_first(left, right):
+    return lax.dot_general(left, right, (((0,), (0,)), ((), ())), preferred_element_type=F32)
+
+
+def expert_kernel(
+    x_ref, dy_ref, wg_ref, wu_ref, wd_ref, route_ref, own_ref,
+    part, from_sib, from_prev, done,
+    s_sib, r_sib, s_rs, r_rs, s_ag, r_ag, s_fin, r_fin,
+):
+    rows, hid = x_ref.shape[0], wg_ref.shape[1]
+    half = rows // 2
+    count = half // (2 * CHUNK)
+    chips = lax.axis_size("dp") // 2
+    last = chips - 1
+    me = lax.axis_index("dp")
+    core = lax.rem(me, 2)
+    chip = lax.div(me, 2)
+    sib = {"dp": me + 1 - 2 * core}
+
+    barrier = pltpu.get_barrier_semaphore()
+    pl.semaphore_signal(barrier, inc=1, device_id=sib, device_id_type=MESH)
+
+    @pl.when(chip > 0)
+    def _():
+        pl.semaphore_signal(barrier, inc=1, device_id={"dp": me - 2}, device_id_type=MESH)
+
+    @pl.when(chip < last)
+    def _():
+        pl.semaphore_signal(barrier, inc=1, device_id={"dp": me + 2}, device_id_type=MESH)
+
+    inner = (chip > 0) & (chip < last)
+
+    @pl.when(inner)
+    def _():
+        pl.semaphore_wait(barrier, 3)
+
+    @pl.when(jnp.logical_not(inner))
+    def _():
+        pl.semaphore_wait(barrier, 2)
+
+    def at(f, k):
+        return pl.multiple_of((f * count + k) * CHUNK, CHUNK)
+
+    def own_rows(f, k):
+        return pl.ds(pl.multiple_of(core * half + at(f, k), CHUNK), CHUNK)
+
+    def sib_rows(f, k):
+        return pl.ds(pl.multiple_of((1 - core) * half + at(f, k), CHUNK), CHUNK)
+
+    def buf_rows(f, k):
+        return pl.ds(at(f, k), CHUNK)
+
+    def send_sib(f, k):
+        return pltpu.make_async_remote_copy(
+            src_ref=part.at[sib_rows(f, k)], dst_ref=from_sib.at[buf_rows(f, k)],
+            send_sem=s_sib.at[f, k], recv_sem=r_sib.at[f, k],
+            device_id=sib, device_id_type=MESH,
+        )
+
+    def send_rs(f, k):
+        nxt = {"dp": me + 2 if f == 0 else me - 2}
+        return pltpu.make_async_remote_copy(
+            src_ref=part.at[own_rows(f, k)], dst_ref=from_prev.at[buf_rows(f, k)],
+            send_sem=s_rs.at[f, k], recv_sem=r_rs.at[f, k],
+            device_id=nxt, device_id_type=MESH,
+        )
+
+    def send_ag(f, k):
+        prev = {"dp": me - 2 if f == 0 else me + 2}
+        return pltpu.make_async_remote_copy(
+            src_ref=done.at[own_rows(f, k)], dst_ref=done.at[own_rows(f, k)],
+            send_sem=s_ag.at[f, k], recv_sem=r_ag.at[f, k],
+            device_id=prev, device_id_type=MESH,
+        )
+
+    def send_fin(f, k):
+        return pltpu.make_async_remote_copy(
+            src_ref=done.at[own_rows(f, k)], dst_ref=done.at[own_rows(f, k)],
+            send_sem=s_fin.at[f, k], recv_sem=r_fin.at[f, k],
+            device_id=sib, device_id_type=MESH,
+        )
+
+    def parts_of(which):
+        here = pl.ds(pl.multiple_of(which * half, CHUNK), half)
+
+        @pl.loop(0, hid // 256)
+        def _(j):
+            cols = pl.ds(pl.multiple_of(j * 256, 256), 256)
+            x = x_ref[here, :]
+            dy = dy_ref[here, :]
+            part[here, pl.ds(pl.multiple_of(j * 256, 256), 256)] = jnp.dot(
+                x, wg_ref[:, cols], preferred_element_type=F32
+            ).astype(BF)
+            part[here, pl.ds(pl.multiple_of(hid + j * 256, 256), 256)] = jnp.dot(
+                x, wu_ref[:, cols], preferred_element_type=F32
+            ).astype(BF)
+            part[here, pl.ds(pl.multiple_of(2 * hid + j * 256, 256), 256)] = dot_last(
+                dy, wd_ref[cols, :]
+            ).astype(BF)
+
+    parts_of(1 - core)
+
+    @pl.loop(0, count)
+    def _(k):
+        for f in range(2):
+            send_sib(f, k).start()
+
+    parts_of(core)
+
+    @pl.loop(0, count + 2 * last)
+    def _(tick):
+        for f in range(2):
+            q = chip if f == 0 else last - chip
+            k = tick - q
+
+            @pl.when((k >= 0) & (k < count))
+            def _():
+                send_sib(f, k).wait_recv()
+                mine = own_rows(f, k)
+
+                @pl.when(q == 0)
+                def _():
+                    for c in range(3):
+                        cols = pl.ds(c * hid, hid)
+                        part[mine, cols] = (
+                            part[mine, cols].astype(F32)
+                            + from_sib[buf_rows(f, k), cols].astype(F32)
+                        ).astype(BF)
+
+                @pl.when(q > 0)
+                def _():
+                    send_rs(f, k).wait_recv()
+
+                @pl.when((q > 0) & (q < last))
+                def _():
+                    for c in range(3):
+                        cols = pl.ds(c * hid, hid)
+                        part[mine, cols] = (
+                            part[mine, cols].astype(F32)
+                            + from_sib[buf_rows(f, k), cols].astype(F32)
+                            + from_prev[buf_rows(f, k), cols].astype(F32)
+                        ).astype(BF)
+
+                @pl.when(q < last)
+                def _():
+                    send_rs(f, k).start()
+
+                @pl.when(q == last)
+                def _():
+                    sums = []
+                    for c in range(3):
+                        cols = pl.ds(c * hid, hid)
+                        sums.append(
+                            part[mine, cols].astype(F32)
+                            + from_sib[buf_rows(f, k), cols].astype(F32)
+                            + from_prev[buf_rows(f, k), cols].astype(F32)
+                        )
+                    for c, value in enumerate(swiglu_back(*sums)):
+                        done[mine, pl.ds(c * hid, hid)] = value
+                    send_ag(f, k).start()
+                    send_fin(f, k).start()
+
+        for f in range(2):
+            q = chip if f == 0 else last - chip
+            k = tick - 2 * last + q
+
+            @pl.when((q < last) & (k >= 0) & (k < count))
+            def _():
+                send_ag(f, k).wait_recv()
+
+                @pl.when(q > 0)
+                def _():
+                    send_ag(f, k).start()
+
+                send_fin(f, k).start()
+
+    @pl.loop(0, count)
+    def _(k):
+        for f in range(2):
+            q = chip if f == 0 else last - chip
+            send_fin(f, k).wait_recv()
+            send_sib(f, k).wait_send()
+            send_fin(f, k).wait_send()
+
+            @pl.when(q < last)
+            def _():
+                send_rs(f, k).wait_send()
+
+            @pl.when(q > 0)
+            def _():
+                send_ag(f, k).wait_send()
+
+    block = rows // 4
+
+    @pl.loop(0, 4)
+    def _(j):
+        here = pl.ds(pl.multiple_of(j * block, 64), block)
+        route_ref[here, :] = (
+            dot_last(done[here, pl.ds(hid, hid)], wg_ref[...])
+            + dot_last(done[here, pl.ds(2 * hid, hid)], wu_ref[...])
+        ).astype(BF)
+
+    @pl.loop(0, hid // 256)
+    def _(j):
+        cols = pl.ds(pl.multiple_of(j * 256, 256), 256)
+        own_ref[cols, :] = dot_first(done[:, cols], dy_ref[...])
+
+
+def expert_call(rows_x, rows_dy, w_gate, w_up, w_down):
+    rows, width = rows_x.shape
+    hid = w_gate.shape[1]
+    half = rows // 2
+    count = half // (2 * CHUNK)
+    sems = [pltpu.SemaphoreType.DMA((2, count))] * 8
+    return pl.pallas_call(
+        expert_kernel,
+        out_shape=(
+            jax.ShapeDtypeStruct((rows, width), BF),
+            jax.ShapeDtypeStruct((hid, width), F32),
+        ),
+        in_specs=[pl.BlockSpec(memory_space=pltpu.VMEM)] * 5,
+        out_specs=[pl.BlockSpec(memory_space=pltpu.VMEM)] * 2,
+        scratch_shapes=[
+            pltpu.VMEM((rows, 3 * hid), BF),
+            pltpu.VMEM((half, 3 * hid), BF),
+            pltpu.VMEM((half, 3 * hid), BF),
+            pltpu.VMEM((rows, 3 * hid), BF),
+        ] + sems,
+        compiler_params=pltpu.CompilerParams(
+            collective_id=0, has_side_effects=True, vmem_limit_bytes=50 * 1024 * 1024
+        ),
+        cost_estimate=pl.CostEstimate(
+            flops=12 * rows * width * hid, bytes_accessed=8 * 1024 * 1024, transcendentals=0
+        ),
+        name="expert_sums",
+    )(rows_x, rows_dy, w_gate, w_up, w_down)
 
 
 def from_partner(block, axis, stride):
@@ -12,23 +272,6 @@
         if high != low and high < count:
             route += [(low, high), (high, low)]
     return lax.ppermute(block, axis, route)
-
-
-def swiglu_back(gate_sum, up_sum, grad_hidden):
-    sigmoid_gate = jax.nn.sigmoid(gate_sum)
-    active = gate_sum * sigmoid_gate
-    hidden = (active * up_sum).astype(jnp.bfloat16)
-    grad_up = (grad_hidden * active).astype(jnp.bfloat16)
-    grad_gate = (
-        grad_hidden * up_sum * sigmoid_gate * (1.0 + gate_sum * (1.0 - sigmoid_gate))
-    ).astype(jnp.bfloat16)
-    return (hidden, grad_gate, grad_up)
-
-
-def contract_last(left, right):
-    return lax.dot_general(
-        left, right, (((1,), (1,)), ((), ())), preferred_element_type=jnp.float32
-    )
 
 
 def contract_first(left, right):
@@ -83,19 +326,7 @@
     gate_weight = w_gate[0]
     up_weight = w_up[0]
     down_weight = w_down[0]
-    gate_part = jnp.dot(rows_x, gate_weight, preferred_element_type=jnp.float32)
-    up_part = jnp.dot(rows_x, up_weight, preferred_element_type=jnp.float32)
-    hidden_part = contract_last(rows_dy, down_weight)
-    gate_part, up_part, hidden_part = (gate_part, up_part, hidden_part)
-    gate_sum, up_sum, grad_hidden = (
-        lax.psum(gate_part.astype(jnp.bfloat16), "dp").astype(jnp.float32),
-        lax.psum(up_part.astype(jnp.bfloat16), "dp").astype(jnp.float32),
-        lax.psum(hidden_part.astype(jnp.bfloat16), "dp").astype(jnp.float32),
-    )
-    hidden, grad_gate, grad_up = swiglu_back(gate_sum, up_sum, grad_hidden)
-    route_grad = (contract_last(grad_gate, gate_weight) + contract_last(grad_up, up_weight)).astype(
-        jnp.bfloat16
-    )
+    route_grad, own_grad = expert_call(rows_x, rows_dy, gate_weight, up_weight, down_weight)
     returned = lax.all_to_all(
         route_grad.reshape(slot_count, capacity, width),
         "expert",
@@ -107,7 +338,6 @@
     grad_tokens = jnp.sum(per_route.reshape(tok_rows, route_count, width), axis=1).astype(
         jnp.bfloat16
     )
-    own_grad = contract_first(hidden, rows_dy)
     pair_bit = slot_count.bit_length() - 2
     half_slots = slot_count // 2
     hot_flag = jnp.any(hot_pairs == lax.axis_index("expert") % half_slots).astype(jnp.float32)

time: 304 us -> 241 us (0.79)
  waiting for transfers between devices: 201 us -> 86.2 us
  Pallas kernels: 0 us -> 94.3 us
  matrix products: 24 us -> 2.4 us
  between operations: 14.9 us -> 1.52 us
  starting transfers between devices: 47.4 us -> 38.3 us
    psum x1 -> x0, waiting for transfers between devices: 124 us -> none  [on_device(): lax.psum(up_part.astype(jnp.bfloat16), 'dp').astype(jnp.float32)]
    pallas_call x0 -> x1, Pallas kernels: none -> 94.3 us  [expert_call(): pl.pallas_call(expert_kernel, out_shape=(jax.ShapeDtypeStruct((rows, widt...]
    dot_general x5 -> x0, matrix products: 14.6 us -> none  [the longest x3 9.02 us: contract_last(): lax.dot_general(left, right, (((1,), (1,)), ((), ())), preferred_element_...]
    all_to_all x1, starting transfers between devices: 15.1 us -> 6.01 us  [on_device(): lax.all_to_all(route_grad.reshape(slot_count, capacity, width), 'expert',...]
    all_to_all x1, waiting for transfers between devices: 21.6 us -> 27.9 us  [on_device(): lax.all_to_all(send_dy, 'expert', split_axis=0, concat_axis=0, tiled=True)]
    dot_general x2 -> x1, matrix products: 7.05 us -> 1.16 us  [contract_first(): lax.dot_general(left, right, (((0,), (0,)), ((), ())), preferred_element_...]
  transfers between devices with their start and end apart: 5 -> 4, of which waited for: 4 -> 3; matrix products, arithmetic and copies ran while one was open for 7% -> 4% of each run, Pallas kernels for 0% -> 0%
where the time goes in v1:
time: 241 us; the launch traced here: 240 us
  Pallas kernels  94.3 us (39%)
  waiting for transfers between devices  86.2 us (36%)
  starting transfers between devices  38.3 us (16%)
  local copies, waits for them, and re-layouts  10.9 us (5%)
  other arithmetic  6.39 us (3%)
    pallas_call x1, Pallas kernels, expert_call(): pl.pallas_call(expert_kernel, out_shape=(jax.ShapeDtypeStruct((rows, widt...  94.3 us
    ppermute x1, waiting for transfers between devices, from_partner(): return lax.ppermute(block, axis, route)  31.2 us
    all_to_all x1, waiting for transfers between devices, on_device(): lax.all_to_all(send_dy, 'expert', split_axis=0, concat_axis=0, tiled=True)  27.9 us
    all_to_all x1, waiting for transfers between devices, on_device(): lax.all_to_all(send_x, 'expert', split_axis=0, concat_axis=0, tiled=True)  27.1 us
    all_to_all x1, starting transfers between devices, on_device(): lax.all_to_all(send_x, 'expert', split_axis=0, concat_axis=0, tiled=True)  19.6 us
    all_to_all x1, starting transfers between devices, on_device(): lax.all_to_all(send_dy, 'expert', split_axis=0, concat_axis=0, tiled=True)  8.24 us
    all_to_all x1, starting transfers between devices, on_device(): lax.all_to_all(route_grad.reshape(slot_count, capacity, width), 'expert',...  6.01 us
  transfers between devices with their start and end apart: 4, of which 3 were waited for; matrix products, arithmetic and copies ran while one was open for 4% of the time, Pallas kernels for 0%

profile of v1, /device:TPU:1, one launch (start us, length us, event | category | flops | bytes accessed | tf_op | source)
XLA Modules:
  0.0 240.0 jit_solution(15411641993623622082)
XLA Ops:
  0.6 0.8 slice_bitcast_fusion.1
  1.4 0.1 broadcast_select_fusion
  1.5 0.7 select_reduce_fusion
  2.2 0.1 copy.16
  2.3 0.1 reshape.141
  2.5 0.1 eq.91
  2.6 1.1 broadcast_in_dim.56
  3.7 0.2 reshape.143
  3.9 0.9 reduce-window.6
  4.8 0.2 slice_reduce_fusion
  5.1 0.1 fusion.7
  5.2 0.6 convolution_convert_fusion.1
  5.8 0.0 copy-start.3
  5.8 1.1 reshape.144
  7.0 19.6 %all-to-all-start = ((bf16[64,12,512]{2,1,0:T(8,128)(2,1)}), bf16[64,12,512]{2,1,0:T(8,128)(2,1)S(1)}, u32[]{:S(2)}, u32[]{:S(2)}) async-start(bf16[64,12,512]{2,1,0:T(8,128)(2,1)} %reshape.144), calls=%async_computation | async-start | bytes 2097152 | tf_op jit(solution)/shard_map/all_to_all | solution.py:321
  26.5 0.0 copy-done.3
  26.6 0.0 copy-start.4
  26.6 0.2 mul.42
  26.8 0.5 mul.43
  27.3 0.0 copy-done.4
  27.3 0.1 copy.19
  27.5 0.1 mul.40
  27.6 0.7 convolution_convert_fusion
  28.3 1.2 reshape.146
  29.5 27.1 %all-to-all-done = bf16[64,12,512]{2,1,0:T(8,128)(2,1)S(1)} async-done(((bf16[64,12,512]{2,1,0:T(8,128)(2,1)}), bf16[64,12,512]{2,1,0:T(8,128)(2,1)S(1)}, u32[]{:S(2)}, u32[]{:S(2)}) %all-to-all-start) | async-done | bytes 786464 | tf_op jit(solution)/shard_map/all_to_all | solution.py:321
  56.6 8.2 %all-to-all-start.1 = ((bf16[64,12,512]{2,1,0:T(8,128)(2,1)}), bf16[64,12,512]{2,1,0:T(8,128)(2,1)}, u32[]{:S(2)}, u32[]{:S(2)}) async-start(bf16[64,12,512]{2,1,0:T(8,128)(2,1)} %reshape.146), calls=%async_computation.1 | async-start | bytes 2097152 | tf_op jit(solution)/shard_map/all_to_all | solution.py:322
  64.9 0.0 copy-start
  64.9 0.2 reshape.145.x_ref
  65.1 27.9 %all-to-all-done.1 = bf16[64,12,512]{2,1,0:T(8,128)(2,1)} async-done(((bf16[64,12,512]{2,1,0:T(8,128)(2,1)}), bf16[64,12,512]{2,1,0:T(8,128)(2,1)}, u32[]{:S(2)}, u32[]{:S(2)}) %all-to-all-start.1) | async-done | bytes 786464 | tf_op jit(solution)/shard_map/all_to_all | solution.py:322
  92.9 1.3 reshape.147.dy_ref
  94.2 0.0 copy-done
  94.2 94.3 %expert_sums.1 = (bf16[768,512]{1,0:T(8,128)(2,1)S(1)}, f32[1024,512]{1,0:T(8,128)}) custom-call(bf16[768,512]{1,0:T(8,128)(2,1)S(1)} %reshape.145.x_ref, bf16[768,512]{1,0:T(8,128)(2,1)S(1)} %reshape.147.dy_ref, bf16[512,1024]{1,0:T(8,128)(2,1)S(1)} %bitcast.31, bf16[512,1024]{1,0:T(8,128)(2,1)} %bitcast.33, bf16[1024,512]{1,0:T(8,128)(2,1)} %bitcast.34), custom_call_target="tpu_custom_call" | custom-call | flops 4831838208 | bytes 8388608 | tf_op jit(solution)/shard_map/expert_sums/pallas_call | solution.py:243
  188.5 1.2 reshape.148
  189.7 0.0 copy-start.1
  189.7 6.0 %all-to-all-start.2 = ((bf16[64,12,512]{2,1,0:T(8,128)(2,1)}), bf16[64,12,512]{2,1,0:T(8,128)(2,1)S(1)}, u32[]{:S(2)}, u32[]{:S(2)}) async-start(bf16[64,12,512]{2,1,0:T(8,128)(2,1)} %reshape.148), calls=%async_computation.2 | async-start | bytes 2097152 | tf_op jit(solution)/shard_map/all_to_all | solution.py:330
  195.7 0.0 copy-done.1
  195.7 0.0 copy-start.5
  195.7 1.1 convert_element_type.45
  196.8 4.5 %collective-permute-start = (bf16[1024,512]{1,0:T(8,128)(2,1)}, bf16[1024,512]{1,0:T(8,128)(2,1)}, u32[]{:S(2)}, u32[]{:S(2)}) collective-permute-start(bf16[1024,512]{1,0:T(8,128)(2,1)} %convert_element_type.45), channel_id=1, source_target_pairs={{0,32},{32,0},{1,33},{33,1},{2,34},{34,2},{3,35},{35,3},{4,36},{36... | collective-permute-start | bytes 3145736 | tf_op jit(solution)/shard_map/ppermute | solution.py:274
  201.4 0.2 iota_compare_fusion.3
  201.6 1.1 eq.97
  202.7 0.0 copy-done.5
  202.7 0.6 compare_reduce_fusion
  204.0 31.2 %collective-permute-done = bf16[1024,512]{1,0:T(8,128)(2,1)} collective-permute-done((bf16[1024,512]{1,0:T(8,128)(2,1)}, bf16[1024,512]{1,0:T(8,128)(2,1)}, u32[]{:S(2)}, u32[]{:S(2)}) %collective-permute-start) | collective-permute-done | bytes 1048608 | tf_op jit(solution)/shard_map/ppermute | solution.py:274
  235.2 2.5 %fusion.1 = bf16[1,1024,512]{2,1,0:T(8,128)(2,1)} fusion(f32[1024,512]{1,0:T(8,128)S(1)} %copy-done.1, bf16[1024,512]{1,0:T(8,128)(2,1)} %collective-permute-done, f32[]{:T(128)S(6)} %convert_element_type.44), kind=kLoop, calls=%fused_computation.7 | loop fusion | flops 2097152 | bytes 4194308 | tf_op jit(solution)/shard_map/broadcast_in_dim | solution.py:345
  237.7 0.0 copy-start.2
  237.7 0.0 all-to-all-done.2
  237.7 0.2 reshape.150
  237.9 0.9 copy-done.2
  238.8 1.2 convolution_reduce_fusion
  (4 shorter events, 0.1 us)
Async XLA Ops:
  5.8 20.7 %copy-start.3 = (bf16[192,512]{1,0:T(8,128)(2,1)S(1)}, bf16[192,512]{1,0:T(8,128)(2,1)}, u32[]{:S(2)}) copy-start(bf16[192,512]{1,0:T(8,128)(2,1)} %param.10) | copy-start | bytes 589828
  7.0 49.6 %all-to-all-start = ((bf16[64,12,512]{2,1,0:T(8,128)(2,1)}), bf16[64,12,512]{2,1,0:T(8,128)(2,1)S(1)}, u32[]{:S(2)}, u32[]{:S(2)}) async-start(bf16[64,12,512]{2,1,0:T(8,128)(2,1)} %reshape.144), calls=%async_computation | async-start | bytes 2097152 | tf_op jit(solution)/shard_map/all_to_all | solution.py:321
  26.6 0.8 copy-start.4
  56.6 36.3 %all-to-all-start.1 = ((bf16[64,12,512]{2,1,0:T(8,128)(2,1)}), bf16[64,12,512]{2,1,0:T(8,128)(2,1)}, u32[]{:S(2)}, u32[]{:S(2)}) async-start(bf16[64,12,512]{2,1,0:T(8,128)(2,1)} %reshape.146), calls=%async_computation.1 | async-start | bytes 2097152 | tf_op jit(solution)/shard_map/all_to_all | solution.py:322
  64.9 29.4 %copy-start = (bf16[1,512,1024]{2,1,0:T(8,128)(2,1)S(1)}, bf16[1,512,1024]{2,1,0:T(8,128)(2,1)}, u32[]{:S(2)}) copy-start(bf16[1,512,1024]{2,1,0:T(8,128)(2,1)} %param.15) | copy-start | bytes 3145732
  189.7 6.0 %copy-start.1 = (f32[1024,512]{1,0:T(8,128)S(1)}, f32[1024,512]{1,0:T(8,128)}, u32[]{:S(2)}) copy-start(f32[1024,512]{1,0:T(8,128)} %get-tuple-element.5) | copy-start | bytes 6291460
  189.7 48.1 %all-to-all-start.2 = ((bf16[64,12,512]{2,1,0:T(8,128)(2,1)}), bf16[64,12,512]{2,1,0:T(8,128)(2,1)S(1)}, u32[]{:S(2)}, u32[]{:S(2)}) async-start(bf16[64,12,512]{2,1,0:T(8,128)(2,1)} %reshape.148), calls=%async_computation.2 | async-start | bytes 2097152 | tf_op jit(solution)/shard_map/all_to_all | solution.py:330
  195.7 7.0 %copy-start.5 = (s32[16]{0:T(128)S(1)}, s32[16]{0:T(128)}, u32[]{:S(2)}) copy-start(s32[16]{0:T(128)} %param.14) | copy-start | bytes 196
  196.8 38.4 %collective-permute-start = (bf16[1024,512]{1,0:T(8,128)(2,1)}, bf16[1024,512]{1,0:T(8,128)(2,1)}, u32[]{:S(2)}, u32[]{:S(2)}) collective-permute-start(bf16[1024,512]{1,0:T(8,128)(2,1)} %convert_element_type.45), channel_id=1, source_target_pairs={{0,32},{32,0},{1,33},{33,1},{2,34},{34,2},{3,35},{35,3},{4,36},{36... | collective-permute-start | bytes 3145736 | tf_op jit(solution)/shard_map/ppermute | solution.py:274
  237.7 1.1 copy-start.2

commit v2 on v1

--- a/solution.py
+++ b/solution.py
@@ -1,5 +1,6 @@
 import jax
 import jax.numpy as jnp
+import numpy as np
 from jax import lax
 from jax.experimental import pallas as pl
 from jax.experimental.pallas import tpu as pltpu
@@ -9,6 +10,10 @@
 F32 = jnp.float32
 MESH = pl.DeviceIdType.MESH
 CHUNK = 32
+PIECE = 48
+CAP = 12
+NX = 4
+NY = 8
 
 
 def swiglu_back(gate_sum, up_sum, grad_hidden):
@@ -264,6 +269,294 @@
     )(rows_x, rows_dy, w_gate, w_up, w_down)
 
 
+def coords():
+    spot = lax.axis_index("expert")
+    dp = lax.axis_index("dp")
+    y = lax.rem(spot, NY)
+    z_hi = lax.rem(lax.div(spot, NY), 2)
+    x = lax.div(spot, 2 * NY)
+    z_lo = lax.div(dp, 2)
+    return x, z_hi, y, z_hi * 4 + z_lo, lax.rem(dp, 2)
+
+
+def at_place(x, y, z, core):
+    return {
+        "dp": lax.rem(z, 4) * 2 + core,
+        "expert": (x * 2 + lax.div(z, 4)) * NY + y,
+    }
+
+
+def plane_target(x, z_hi, y):
+    return {"expert": (x * 2 + z_hi) * NY + y}
+
+
+def signal_all(barrier, places):
+    for place in places:
+        pl.semaphore_signal(barrier, inc=1, device_id=place, device_id_type=MESH)
+
+
+def signal_plane(barrier, x, z_hi, y):
+    @pl.loop(1, NX * NY)
+    def _(step):
+        there = lax.rem(x * NY + y + step, NX * NY)
+        pl.semaphore_signal(
+            barrier, inc=1,
+            device_id=plane_target(lax.div(there, NY), z_hi, lax.rem(there, NY)),
+            device_id_type=MESH,
+        )
+
+
+def column_of(row):
+    n = row.shape[1]
+    diagonal = lax.broadcasted_iota(jnp.int32, (n, n), 0) == lax.broadcasted_iota(
+        jnp.int32, (n, n), 1
+    )
+    return jnp.sum(jnp.where(diagonal, row, 0.0), axis=1, keepdims=True)
+
+
+def route_targets(ids_ref, slots_ref, slot_count, capacity):
+    tok = ids_ref.shape[1]
+    experts = slots_ref.shape[0]
+    odd = lax.broadcasted_iota(jnp.int32, (experts, tok), 1) % 2 == 1
+    table = jnp.where(odd, slots_ref[:, 1:2], slots_ref[:, 0:1])
+    expert_row = lax.broadcasted_iota(jnp.int32, (experts, tok), 0)
+    slot_row = lax.broadcasted_iota(jnp.int32, (slot_count, tok), 0)
+    slots = [
+        jnp.sum(jnp.where(ids_ref[k : k + 1, :] == expert_row, table, 0), axis=0, keepdims=True)
+        for k in range(2)
+    ]
+    hits = [jnp.where(slot == slot_row, 1.0, 0.0) for slot in slots]
+    earlier = lax.broadcasted_iota(jnp.int32, (tok, tok), 0) < lax.broadcasted_iota(
+        jnp.int32, (tok, tok), 1
+    )
+    before = jnp.dot(
+        (hits[0] + hits[1]).astype(BF),
+        jnp.where(earlier, 1.0, 0.0).astype(BF),
+        preferred_element_type=F32,
+    )
+    return [
+        slot.astype(F32) * capacity + jnp.sum(hit * before, axis=0, keepdims=True)
+        for slot, hit in zip(slots, hits)
+    ]
+
+
+def dispatch_kernel(
+    tok_ref, cot_ref, scale_ref, ids_ref, slots_ref, codes_ref, perm_ref,
+    rows_x_ref, rows_dy_ref,
+    relay, far, meta, far_meta, scaled, send, land,
+    s_one, r_one, s_two, r_two, s_meta, r_meta, s_xy, r_xy,
+):
+    tok, width = tok_ref.shape
+    slot_count = NX * 2 * NY
+    capacity = CAP
+    wide = width // 2
+    message = 4 * capacity
+    x, z_hi, y, z, core = coords()
+    plane = NX * NY
+    here = x * NY + y
+    up = at_place(x, y, lax.rem(z + 2, 8), core)
+    down = at_place(x, y, lax.rem(z + 6, 8), core)
+    across = at_place(x, y, lax.rem(z + 4, 8), core)
+    pieces = tok // PIECE
+
+    barrier = pltpu.get_barrier_semaphore()
+    signal_all(barrier, (up, down, across))
+    signal_plane(barrier, x, z_hi, y)
+    targets = route_targets(ids_ref, slots_ref, slot_count, capacity)
+    meta[...] = jnp.zeros_like(meta)
+    for k in range(2):
+        meta[k : k + 1, 0:tok] = targets[k]
+        meta[k + 2 : k + 3, 0:tok] = scale_ref[k : k + 1, :]
+    pl.semaphore_wait(barrier, plane - 1 + 3)
+
+    def leg_one(d, p):
+        rows = pl.ds(p * PIECE, PIECE)
+        source = tok_ref if d == 0 else cot_ref
+        return pltpu.make_async_remote_copy(
+            src_ref=source.at[rows], dst_ref=relay.at[d, rows],
+            send_sem=s_one.at[d, p], recv_sem=r_one.at[d, p],
+            device_id=up if d == 0 else down, device_id_type=MESH,
+        )
+
+    def leg_two(d, p):
+        rows = pl.ds(p * PIECE, PIECE)
+        return pltpu.make_async_remote_copy(
+            src_ref=relay.at[d, rows], dst_ref=far.at[d, rows],
+            send_sem=s_two.at[d, p], recv_sem=r_two.at[d, p],
+            device_id=up if d == 0 else down, device_id_type=MESH,
+        )
+
+    meta_copy = pltpu.make_async_remote_copy(
+        src_ref=meta, dst_ref=far_meta, send_sem=s_meta, recv_sem=r_meta,
+        device_id=across, device_id_type=MESH,
+    )
+    for p in range(pieces):
+        for d in range(2):
+            leg_one(d, p).start()
+    meta_copy.start()
+
+    def to_plane(s, there):
+        rows = pl.multiple_of((s * plane + there) * message, 16)
+        into = pl.multiple_of((s * plane + here) * message, 16)
+        return pltpu.make_async_remote_copy(
+            src_ref=send.at[pl.ds(rows, message)], dst_ref=land.at[pl.ds(into, message)],
+            send_sem=s_xy.at[s, there], recv_sem=r_xy.at[s, here],
+            device_id=plane_target(lax.div(there, NY), z_hi, lax.rem(there, NY)),
+            device_id_type=MESH,
+        )
+
+    def to_self(s):
+        rows = pl.multiple_of((s * plane + here) * message, 16)
+        return pltpu.make_async_copy(
+            send.at[pl.ds(rows, message)], land.at[pl.ds(rows, message)], r_xy.at[s, here]
+        )
+
+    def from_plane(s, there):
+        rows = pl.multiple_of((s * plane + there) * message, 16)
+        return pltpu.make_async_remote_copy(
+            src_ref=send.at[pl.ds(rows, message)], dst_ref=land.at[pl.ds(rows, message)],
+            send_sem=s_xy.at[s, there], recv_sem=r_xy.at[s, there],
+            device_id=plane_target(lax.div(there, NY), z_hi, lax.rem(there, NY)),
+            device_id_type=MESH,
+        )
+
+    pairs = NY // 2
+    band = pairs * message
+
+    def build(s, tok_view, cot_view, info):
+        for k in range(2):
+            scaled[k, ...] = (column_of(info[k + 2 : k + 3, 0:tok]) * cot_view[...].astype(F32)).astype(BF)
+
+        @pl.loop(0, NX)
+        def _(step):
+            to_x = lax.rem(x + 2 + step, NX)
+            for k in range(2):
+                base = (to_x * 2 + z_hi) * (NY * capacity) + k * capacity
+                want = info[k : k + 1, 0:tok] - base.astype(F32)
+                total = None
+                for p in range(4):
+                    source = tok_view if p < 2 else scaled.at[k]
+                    cols = pl.ds((p % 2) * wide, wide)
+                    chosen = jnp.where(codes_ref[:, p : p + 1] == want, 1.0, 0.0).astype(BF)
+                    term = jnp.dot(chosen, source[:, cols], preferred_element_type=F32)
+                    total = term if total is None else total + term
+                for yy in range(pairs):
+                    rows = (s * plane + to_x * NY + 2 * yy + k) * message
+                    send[pl.ds(pl.multiple_of(rows, 16), message), :] = total[
+                        yy * message : (yy + 1) * message
+                    ].astype(BF)
+            for to_y in range(NY):
+                there = to_x * NY + to_y
+
+                @pl.when(there != here)
+                def _():
+                    to_plane(s, there).start()
+
+                @pl.when(there == here)
+                def _():
+                    to_self(s).start()
+
+    build(0, tok_ref, cot_ref, meta)
+    for p in range(pieces):
+        for d in range(2):
+            leg_one(d, p).wait_recv()
+            leg_two(d, p).start()
+    meta_copy.wait_recv()
+    for p in range(pieces):
+        for d in range(2):
+            leg_two(d, p).wait_recv()
+    build(1, far.at[0], far.at[1], far_meta)
+
+    group = 4 * message
+    block = 4 * capacity
+
+    @pl.loop(0, 2 * plane // 4)
+    def _(g):
+        s = lax.div(g, plane // 4)
+        first = lax.rem(g, plane // 4) * 4
+        for j in range(4):
+            there = first + j
+
+            @pl.when(there != here)
+            def _():
+                from_plane(s, there).wait_recv()
+
+            @pl.when(there == here)
+            def _():
+                to_self(s).wait()
+
+        rows = land[pl.ds(pl.multiple_of(g * group, 16), group), :]
+        out = jnp.dot(perm_ref[...], rows, preferred_element_type=F32).astype(BF)
+        into = pl.ds(pl.multiple_of(g * block, 16), block)
+        rows_x_ref[into, 0:wide] = out[0:block]
+        rows_x_ref[into, wide:width] = out[block : 2 * block]
+        rows_dy_ref[into, 0:wide] = out[2 * block : 3 * block]
+        rows_dy_ref[into, wide:width] = out[3 * block : 4 * block]
+
+    for p in range(pieces):
+        for d in range(2):
+            leg_one(d, p).wait_send()
+            leg_two(d, p).wait_send()
+    meta_copy.wait_send()
+
+    @pl.loop(1, plane)
+    def _(step):
+        there = lax.rem(here + step, plane)
+        for s in range(2):
+            to_plane(s, there).wait_send()
+
+
+def message_codes():
+    pairs = NY // 2
+    row = np.arange(pairs * 4 * CAP)
+    pair, inside = row // (4 * CAP), row % (4 * CAP)
+    part, rank = inside // CAP, inside % CAP
+    code = (2 * pair) * CAP + rank
+    return np.where(part[:, None] == np.arange(4)[None, :], code[:, None], -1e6).astype(np.float32)
+
+
+def unfold_order():
+    order = np.arange(16 * CAP).reshape(4, 4, CAP).transpose(1, 0, 2).reshape(-1)
+    return np.eye(16 * CAP, dtype=np.float32)[order]
+
+
+def dispatch_call(tokens, cotangent, gate_scale, expert_ids, expert_slots):
+    tok, width = tokens.shape
+    rows = NX * 2 * NY * CAP
+    message = 4 * CAP
+    plane = NX * NY
+    wide = width // 2
+    pieces = tok // PIECE
+    dma = pltpu.SemaphoreType.DMA
+    return pl.pallas_call(
+        dispatch_kernel,
+        out_shape=(jax.ShapeDtypeStruct((rows, width), BF),) * 2,
+        in_specs=[pl.BlockSpec(memory_space=pltpu.VMEM)] * 7,
+        out_specs=[pl.BlockSpec(memory_space=pltpu.VMEM)] * 2,
+        scratch_shapes=[
+            pltpu.VMEM((2, tok, width), BF),
+            pltpu.VMEM((2, tok, width), BF),
+            pltpu.VMEM((8, 256), F32),
+            pltpu.VMEM((8, 256), F32),
+            pltpu.VMEM((2, tok, width), BF),
+            pltpu.VMEM((2 * plane * message, wide), BF),
+            pltpu.VMEM((2 * plane * message, wide), BF),
+            dma((2, pieces)), dma((2, pieces)), dma((2, pieces)), dma((2, pieces)),
+            dma, dma, dma((2, plane)), dma((2, plane)),
+        ],
+        compiler_params=pltpu.CompilerParams(
+            collective_id=1, has_side_effects=True, vmem_limit_bytes=40 * 1024 * 1024
+        ),
+        cost_estimate=pl.CostEstimate(
+            flops=4 * rows * tok * width * 4, bytes_accessed=4 * 1024 * 1024, transcendentals=0
+        ),
+        name="dispatch",
+    )(
+        tokens, cotangent, gate_scale.T, expert_ids.T, expert_slots,
+        jnp.asarray(message_codes()), jnp.asarray(unfold_order(), dtype=BF),
+    )
+
+
 def from_partner(block, axis, stride):
     count = lax.axis_size(axis)
     route = []
@@ -299,34 +592,12 @@
     placing = (
         jnp.arange(slot_count * capacity, dtype=jnp.int32)[:, None] == target[None, :]
     ).astype(jnp.bfloat16)
-    repeated = jnp.broadcast_to(tokens[:, None, :], (tok_rows, route_count, width)).reshape(
-        entries, width
-    )
-    scaled = (
-        (gate_scale[:, :, None] * cotangent[:, None, :].astype(jnp.float32))
-        .astype(jnp.bfloat16)
-        .reshape(entries, width)
-    )
-    send_x = (
-        jnp.dot(placing, repeated, preferred_element_type=jnp.float32)
-        .astype(jnp.bfloat16)
-        .reshape(slot_count, capacity, width)
-    )
-    send_dy = (
-        jnp.dot(placing, scaled, preferred_element_type=jnp.float32)
-        .astype(jnp.bfloat16)
-        .reshape(slot_count, capacity, width)
-    )
-    recv_x, recv_dy = (
-        lax.all_to_all(send_x, "expert", split_axis=0, concat_axis=0, tiled=True),
-        lax.all_to_all(send_dy, "expert", split_axis=0, concat_axis=0, tiled=True),
-    )
-    rows_x = recv_x.reshape(-1, width)
-    rows_dy = recv_dy.reshape(-1, width)
-    gate_weight = w_gate[0]
-    up_weight = w_up[0]
-    down_weight = w_down[0]
-    route_grad, own_grad = expert_call(rows_x, rows_dy, gate_weight, up_weight, down_weight)
+    rows_x, rows_dy = dispatch_call(tokens, cotangent, gate_scale, expert_ids, expert_slots)
+    route_grad, own_grad = expert_call(rows_x, rows_dy, w_gate[0], w_up[0], w_down[0])
+    z_hi = lax.axis_index("expert") // NY % 2
+    sides = route_grad.reshape(2, NX, NY * CAP, width)
+    sides = jnp.where(z_hi == 1, sides[::-1], sides)
+    route_grad = jnp.transpose(sides, (1, 0, 2, 3))
     returned = lax.all_to_all(
         route_grad.reshape(slot_count, capacity, width),
         "expert",

time: 241 us -> 208 us (0.86)
  waiting for transfers between devices: 86.2 us -> 29.3 us
  Pallas kernels: 94.3 us -> 147 us
  starting transfers between devices: 38.3 us -> 13.3 us
    all_to_all x2 -> x0, waiting for transfers between devices: 55 us -> none  [the longest x1 27.9 us: on_device(): lax.all_to_all(send_dy, 'expert', split_axis=0, concat_axis=0, tiled=True)]
    pallas_call x0 -> x1, Pallas kernels: none -> 53.9 us  [dispatch_call(): pl.pallas_call(dispatch_kernel, out_shape=(jax.ShapeDtypeStruct((rows, wi...]
    all_to_all x2 -> x0, starting transfers between devices: 27.8 us -> none  [the longest x1 19.6 us: on_device(): lax.all_to_all(send_x, 'expert', split_axis=0, concat_axis=0, tiled=True)]
    unnamed x13 -> x23, local copies, waits for them, and re-layouts: 1.03 us -> 5.79 us
    reshape x5 -> x1, local copies, waits for them, and re-layouts: 3.97 us -> 0.07 us  [on_device(): sides = route_grad.reshape(2, NX, NY * CAP, width)]
    all_to_all x1, starting transfers between devices: 6.01 us -> 8.75 us  [on_device(): lax.all_to_all(route_grad.reshape(slot_count, capacity, width), 'expert',...]
  transfers between devices with their start and end apart: 4 -> 2, of which waited for: 3 -> 1; matrix products, arithmetic and copies ran while one was open for 4% -> 4% of each run, Pallas kernels for 0% -> 0%
where the time goes in v2:
time: 208 us
  Pallas kernels  147 us (71%)
  waiting for transfers between devices  29.3 us (14%)
  starting transfers between devices  13.3 us (6%)
  local copies, waits for them, and re-layouts  8.95 us (4%)
  other arithmetic  5.86 us (3%)
  matrix products  2.27 us (1%)
    pallas_call x1, Pallas kernels, expert_call(): pl.pallas_call(expert_kernel, out_shape=(jax.ShapeDtypeStruct((rows, widt...  92.8 us
    pallas_call x1, Pallas kernels, dispatch_call(): pl.pallas_call(dispatch_kernel, out_shape=(jax.ShapeDtypeStruct((rows, wi...  53.9 us
    ppermute x1, waiting for transfers between devices, from_partner(): return lax.ppermute(block, axis, route)  29.3 us
    all_to_all x1, starting transfers between devices, on_device(): lax.all_to_all(route_grad.reshape(slot_count, capacity, width), 'expert',...  8.75 us
    unnamed x23, local copies, waits for them, and re-layouts  5.79 us
    ppermute x1, starting transfers between devices, from_partner(): return lax.ppermute(block, axis, route)  4.51 us
  transfers between devices with their start and end apart: 2, of which 1 were waited for; matrix products, arithmetic and copies ran while one was open for 4% of the time, Pallas kernels for 0%

profile of v2, /device:TPU:1, one launch (start us, length us, event | category | flops | bytes accessed | tf_op | source)
XLA Modules:
  0.0 207.8 jit_solution(6133903658474239561)
XLA Ops:
  0.7 0.8 copy.24.slots_ref
  1.4 0.0 copy-start
  1.4 0.7 copy-done
  2.1 0.0 copy-start.3
  2.1 0.9 copy-done.3
  3.0 0.0 copy-start.4
  3.0 0.9 copy-done.4
  4.0 0.0 copy-start.5
  4.0 0.7 copy-done.5
  4.6 0.0 copy-start.6
  4.6 0.9 copy-done.6
  5.5 0.0 copy-start.7
  5.5 0.9 copy-done.7
  6.4 0.0 copy-start.2
  6.4 53.9 %dispatch.1 = (bf16[768,512]{1,0:T(8,128)(2,1)S(1)}, bf16[768,512]{1,0:T(8,128)(2,1)S(1)}) custom-call(bf16[192,512]{1,0:T(8,128)(2,1)S(1)} %copy-done.3, bf16[192,512]{1,0:T(8,128)(2,1)S(1)} %copy-done.4, f32[2,192]{1,0:T(2,128)S(1)} %bitcast.40, s32[2,192]{1,0:T(2,128)S(1)} %bitcast.38, s32[48,2]{1,0:T(8,128)S(1)} %copy.24.slots_ref, ...), custom_call_target="tpu_custom_call" | custom-call | flops 1207959552 | bytes 4194304 | tf_op jit(solution)/shard_map/dispatch/pallas_call | solution.py:531
  60.3 0.0 copy-done.2
  60.4 92.8 %expert_sums.1 = (bf16[768,512]{1,0:T(8,128)(2,1)S(1)}, f32[1024,512]{1,0:T(8,128)}) custom-call(bf16[768,512]{1,0:T(8,128)(2,1)S(1)} %get-tuple-element.6.x_ref, bf16[768,512]{1,0:T(8,128)(2,1)S(1)} %get-tuple-element.7.dy_ref, bf16[512,1024]{1,0:T(8,128)(2,1)S(1)} %bitcast.39, bf16[512,1024]{1,0:T(8,128)(2,1)} %bitcast.42, bf16[1024,512]{1,0:T(8,128)(2,1)} %bitcast.43), custom_call_target="tpu_custom_call" | custom-call | flops 4831838208 | bytes 8388608 | tf_op jit(solution)/shard_map/expert_sums/pallas_call | solution.py:248
  153.1 0.1 copy.25
  153.2 0.2 fusion.2
  153.4 0.0 copy-start.8
  153.4 1.2 reshape.124
  154.5 8.8 %all-to-all-start = ((bf16[64,12,512]{2,1,0:T(8,128)(2,1)}), bf16[64,12,512]{2,1,0:T(8,128)(2,1)S(1)}, u32[]{:S(2)}, u32[]{:S(2)}) async-start(bf16[64,12,512]{2,1,0:T(8,128)(2,1)} %reshape.124), calls=%async_computation | async-start | bytes 2097152 | tf_op jit(solution)/shard_map/all_to_all | solution.py:601
  163.3 0.0 copy-start.9
  163.3 0.0 copy-start.1
  163.3 0.0 copy-done.8
  163.3 0.0 copy-start.10
  163.3 1.1 convert_element_type.27
  164.5 4.5 %collective-permute-start = (bf16[1024,512]{1,0:T(8,128)(2,1)}, bf16[1024,512]{1,0:T(8,128)(2,1)}, u32[]{:S(2)}, u32[]{:S(2)}) collective-permute-start(bf16[1024,512]{1,0:T(8,128)(2,1)} %convert_element_type.27), channel_id=1, source_target_pairs={{0,32},{32,0},{1,33},{33,1},{2,34},{34,2},{3,35},{35,3},{4,36},{36... | collective-permute-start | bytes 3145736 | tf_op jit(solution)/shard_map/ppermute | solution.py:567
  169.0 0.0 copy-done.9
  169.0 0.1 broadcast_select_fusion
  169.1 0.0 copy-done.1
  169.1 0.1 copy.21
  169.3 0.1 reshape.121
  169.4 0.1 eq.89
  169.6 0.9 reduce-window.6
  170.5 0.2 slice_reduce_fusion
  170.7 0.1 fusion.5
  170.9 0.2 iota_compare_fusion
  171.1 1.1 eq.95
  172.2 0.0 copy-done.10
  172.2 0.6 compare_reduce_fusion
  173.5 29.3 %collective-permute-done = bf16[1024,512]{1,0:T(8,128)(2,1)} collective-permute-done((bf16[1024,512]{1,0:T(8,128)(2,1)}, bf16[1024,512]{1,0:T(8,128)(2,1)}, u32[]{:S(2)}, u32[]{:S(2)}) %collective-permute-start) | collective-permute-done | bytes 1048608 | tf_op jit(solution)/shard_map/ppermute | solution.py:567
  202.8 2.5 %fusion.1 = bf16[1,1024,512]{2,1,0:T(8,128)(2,1)} fusion(f32[1024,512]{1,0:T(8,128)S(1)} %copy-done.8, bf16[1024,512]{1,0:T(8,128)(2,1)} %collective-permute-done, f32[]{:T(128)S(6)} %convert_element_type.26), kind=kLoop, calls=%fused_computation.5 | loop fusion | flops 2097152 | bytes 4194308 | tf_op jit(solution)/shard_map/broadcast_in_dim | solution.py:616
  205.4 0.0 all-to-all-done
  205.4 0.2 reshape.126
  205.5 2.3 %convolution_reduce_fusion = bf16[192,512]{1,0:T(8,128)(2,1)} fusion(bf16[768,512,1]{1,0,2:T(8,128)(2,1)S(1)} %reshape.126, pred[192,2,768]{2,1,0:T(4,128)(4,1)} %eq.95), kind=kOutput, calls=%fused_computation.1 | convolution fusion | flops 302088192 | bytes 1277952 | tf_op jit(solution)/shard_map/dot_general | solution.py:571
  (6 shorter events, 0.1 us)
Async XLA Ops:
  1.4 0.7 copy-start
  2.1 0.9 copy-start.3
  3.0 0.9 copy-start.4
  4.0 0.7 copy-start.5
  4.6 0.9 copy-start.6
  5.5 0.9 copy-start.7
  6.4 53.9 %copy-start.2 = (bf16[1,512,1024]{2,1,0:T(8,128)(2,1)S(1)}, bf16[1,512,1024]{2,1,0:T(8,128)(2,1)}, u32[]{:S(2)}) copy-start(bf16[1,512,1024]{2,1,0:T(8,128)(2,1)} %param.17) | copy-start | bytes 3145732
  153.4 10.0 %copy-start.8 = (f32[1024,512]{1,0:T(8,128)S(1)}, f32[1024,512]{1,0:T(8,128)}, u32[]{:S(2)}) copy-start(f32[1024,512]{1,0:T(8,128)} %get-tuple-element.9) | copy-start | bytes 6291460
  154.5 50.8 %all-to-all-start = ((bf16[64,12,512]{2,1,0:T(8,128)(2,1)}), bf16[64,12,512]{2,1,0:T(8,128)(2,1)S(1)}, u32[]{:S(2)}, u32[]{:S(2)}) async-start(bf16[64,12,512]{2,1,0:T(8,128)(2,1)} %reshape.124), calls=%async_computation | async-start | bytes 2097152 | tf_op jit(solution)/shard_map/all_to_all | solution.py:601
  163.3 5.7 %copy-start.9 = (s32[48,2]{0,1:T(2,128)S(1)}, s32[48,2]{0,1:T(2,128)}, u32[]{:S(2)}) copy-start(s32[48,2]{0,1:T(2,128)} %param.15) | copy-start | bytes 1156
  163.3 5.8 %copy-start.1 = (s32[192,2]{0,1:T(2,128)S(1)}, s32[192,2]{0,1:T(2,128)}, u32[]{:S(2)}) copy-start(s32[192,2]{0,1:T(2,128)} %param.14) | copy-start | bytes 4612
  163.3 8.9 %copy-start.10 = (s32[16]{0:T(128)S(1)}, s32[16]{0:T(128)}, u32[]{:S(2)}) copy-start(s32[16]{0:T(128)} %param.16) | copy-start | bytes 196
  164.5 38.4 %collective-permute-start = (bf16[1024,512]{1,0:T(8,128)(2,1)}, bf16[1024,512]{1,0:T(8,128)(2,1)}, u32[]{:S(2)}, u32[]{:S(2)}) collective-permute-start(bf16[1024,512]{1,0:T(8,128)(2,1)} %convert_element_type.27), channel_id=1, source_target_pairs={{0,32},{32,0},{1,33},{33,1},{2,34},{34,2},{3,35},{35,3},{4,36},{36... | collective-permute-start | bytes 3145736 | tf_op jit(solution)/shard_map/ppermute | solution.py:567

commit v3 on v0

v3 whole, which is shorter than its diff:
```python
import jax
import jax.numpy as jnp
import numpy as np
from jax import lax
from jax.experimental import pallas as pl
from jax.experimental.pallas import tpu as pltpu
from jax.sharding import PartitionSpec as P

BF = jnp.bfloat16
F32 = jnp.float32
MESH = pl.DeviceIdType.MESH
CAP = 12
NX = 4
NY = 8
BLOCK = 256


def swiglu_back(gate_sum, up_sum, grad_hidden):
    sigmoid_gate = jax.nn.sigmoid(gate_sum)
    active = gate_sum * sigmoid_gate
    hidden = (active * up_sum).astype(BF)
    grad_up = (grad_hidden * active).astype(BF)
    grad_gate = (
        grad_hidden * up_sum * sigmoid_gate * (1.0 + gate_sum * (1.0 - sigmoid_gate))
    ).astype(BF)
    return (hidden, grad_gate, grad_up)


def dot_last(left, right):
    return lax.dot_general(left, right, (((1,), (1,)), ((), ())), preferred_element_type=F32)


def dot_first(left, right):
    return lax.dot_general(left, right, (((0,), (0,)), ((), ())), preferred_element_type=F32)


def coords():
    spot = lax.axis_index("expert")
    dp = lax.axis_index("dp")
    y = lax.rem(spot, NY)
    z_hi = lax.rem(lax.div(spot, NY), 2)
    x = lax.div(spot, 2 * NY)
    z_lo = lax.div(dp, 2)
    return x, z_hi, y, z_hi * 4 + z_lo, lax.rem(dp, 2)


def at_place(x, y, z, core):
    return {
        "dp": lax.rem(z, 4) * 2 + core,
        "expert": (x * 2 + lax.div(z, 4)) * NY + y,
    }


def plane_target(x, z_hi, y):
    return {"expert": (x * 2 + z_hi) * NY + y}


def signal_all(barrier, places):
    for place in places:
        pl.semaphore_signal(barrier, inc=1, device_id=place, device_id_type=MESH)


def signal_plane(barrier, x, z_hi, y):
    @pl.loop(1, NX * NY)
    def _(step):
        there = lax.rem(x * NY + y + step, NX * NY)
        pl.semaphore_signal(
            barrier, inc=1,
            device_id=plane_target(lax.div(there, NY), z_hi, lax.rem(there, NY)),
            device_id_type=MESH,
        )


def column_of(row):
    n = row.shape[1]
    diagonal = lax.broadcasted_iota(jnp.int32, (n, n), 0) == lax.broadcasted_iota(
        jnp.int32, (n, n), 1
    )
    return jnp.sum(jnp.where(diagonal, row, 0.0), axis=1, keepdims=True)


def route_targets(ids_ref, slots_ref, slot_count, capacity):
    tok = ids_ref.shape[1]
    experts = slots_ref.shape[0]
    odd = lax.broadcasted_iota(jnp.int32, (experts, tok), 1) % 2 == 1
    table = jnp.where(odd, slots_ref[:, 1:2], slots_ref[:, 0:1])
    expert_row = lax.broadcasted_iota(jnp.int32, (experts, tok), 0)
    slot_row = lax.broadcasted_iota(jnp.int32, (slot_count, tok), 0)
    slots = [
        jnp.sum(jnp.where(ids_ref[k : k + 1, :] == expert_row, table, 0), axis=0, keepdims=True)
        for k in range(2)
    ]
    hits = [jnp.where(slot == slot_row, 1.0, 0.0) for slot in slots]
    earlier = lax.broadcasted_iota(jnp.int32, (tok, tok), 0) < lax.broadcasted_iota(
        jnp.int32, (tok, tok), 1
    )
    before = jnp.dot(
        (hits[0] + hits[1]).astype(BF),
        jnp.where(earlier, 1.0, 0.0).astype(BF),
        preferred_element_type=F32,
    )
    return [
        slot.astype(F32) * capacity + jnp.sum(hit * before, axis=0, keepdims=True)
        for slot, hit in zip(slots, hits)
    ]


def layer_kernel(
    tok_ref, cot_ref, scale_ref, ids_ref, slots_ref, hot_ref, fold_ref, wg_ref, wu_ref, wd_ref,
    grad_tok_ref, grad_down_ref,
    far, meta, far_meta, gather_x, gather_dy, send, land, rows_x, rows_dy,
    part, from_sib, from_prev, done, route, back_send, back_land, returned,
    partial, cross_send, cross_land, own, pair_send, pair_land,
    s_z, r_z, s_meta, r_meta, s_xy, r_xy, s_sib, r_sib, s_rs, r_rs, s_ag, r_ag, s_fin, r_fin,
    s_back, r_back, s_cross, r_cross, s_pair, r_pair,
):
    tok, width = tok_ref.shape
    hid = wg_ref.shape[1]
    blocks = hid // BLOCK
    plane = NX * NY
    side_rows = plane * CAP
    message = 4 * CAP
    group = 4 * message
    wide, thin = width // 2, width // 4
    part_rows = side_rows // 4
    count = 2 * blocks
    x, z_hi, y, z, core = coords()
    here = x * NY + y
    spot = lax.axis_index("expert")
    me = lax.axis_index("dp")
    chip = lax.div(me, 2)
    last = lax.axis_size("dp") // 2 - 1
    sib = {"dp": me + 1 - 2 * core}
    across = at_place(x, y, lax.rem(z + 4, 8), core)
    pair = {"expert": lax.rem(spot + plane, 2 * plane)}
    inner = (chip > 0) & (chip < last)

    barrier = pltpu.get_barrier_semaphore()
    signal_all(barrier, (across, sib))
    signal_plane(barrier, x, z_hi, y)

    @pl.when(chip > 0)
    def _():
        signal_all(barrier, ({"dp": me - 2},))

    @pl.when(chip < last)
    def _():
        signal_all(barrier, ({"dp": me + 2},))

    targets = route_targets(ids_ref, slots_ref, 2 * plane, CAP)
    meta[...] = jnp.zeros_like(meta)
    for k in range(2):
        meta[k : k + 1, 0:tok] = targets[k]
        meta[k + 2 : k + 3, 0:tok] = scale_ref[k : k + 1, :]

    @pl.when(inner)
    def _():
        pl.semaphore_wait(barrier, plane + 3)

    @pl.when(jnp.logical_not(inner))
    def _():
        pl.semaphore_wait(barrier, plane + 2)

    def crossing(d):
        source = tok_ref if d == 0 else cot_ref
        return pltpu.make_async_remote_copy(
            src_ref=source, dst_ref=far.at[d], send_sem=s_z.at[d], recv_sem=r_z.at[d],
            device_id=across, device_id_type=MESH,
        )

    meta_copy = pltpu.make_async_remote_copy(
        src_ref=meta, dst_ref=far_meta, send_sem=s_meta, recv_sem=r_meta,
        device_id=across, device_id_type=MESH,
    )
    meta_copy.start()
    crossing(0).start()
    crossing(1).start()

    def place_rows(s, there):
        return pl.ds(pl.multiple_of((s * plane + there) * message, 16), message)

    def to_plane(source, into, s, there, sent, got):
        return pltpu.make_async_remote_copy(
            src_ref=source.at[place_rows(s, there)], dst_ref=into.at[place_rows(s, here)],
            send_sem=sent.at[s, there], recv_sem=got.at[s, here],
            device_id=plane_target(lax.div(there, NY), z_hi, lax.rem(there, NY)),
            device_id_type=MESH,
        )

    def from_plane(source, into, s, there, sent, got):
        return pltpu.make_async_remote_copy(
            src_ref=source.at[place_rows(s, there)], dst_ref=into.at[place_rows(s, there)],
            send_sem=sent.at[s, there], recv_sem=got.at[s, there],
            device_id=plane_target(lax.div(there, NY), z_hi, lax.rem(there, NY)),
            device_id_type=MESH,
        )

    def to_self(source, into, s, got):
        return pltpu.make_async_copy(
            source.at[place_rows(s, here)], into.at[place_rows(s, here)], got.at[s, here]
        )

    def start_plane(source, into, s, there, sent, got):
        @pl.when(there != here)
        def _():
            to_plane(source, into, s, there, sent, got).start()

        @pl.when(there == here)
        def _():
            to_self(source, into, s, got).start()

    def wait_plane(source, into, s, there, sent, got):
        @pl.when(there != here)
        def _():
            from_plane(source, into, s, there, sent, got).wait_recv()

        @pl.when(there == here)
        def _():
            to_self(source, into, s, got).wait()

    def row_codes(shape, axis):
        row = lax.broadcasted_iota(jnp.int32, shape, axis)
        band = NY * CAP
        code = row + z_hi * band
        for edge in range(1, NX):
            code = code + jnp.where(row >= edge * band, band, 0)
        return code

    def dispatch(s, tok_view, cot_view, info):
        codes = row_codes((side_rows, tok), 0)
        hits = [
            jnp.where(codes == info[k : k + 1, 0:tok].astype(jnp.int32), 1.0, 0.0).astype(BF)
            for k in range(2)
        ]
        gather_x[...] = jnp.dot(
            hits[0] + hits[1], tok_view[...], preferred_element_type=F32
        ).astype(BF)
        cot = cot_view[...].astype(F32)
        scaled = [
            (column_of(info[k + 2 : k + 3, 0:tok]) * cot).astype(BF) for k in range(2)
        ]
        gather_dy[...] = (
            jnp.dot(hits[0], scaled[0], preferred_element_type=F32)
            + jnp.dot(hits[1], scaled[1], preferred_element_type=F32)
        ).astype(BF)

        @pl.loop(0, plane // 4)
        def _(step):
            g = lax.rem(step + 2 * x + plane // 8, plane // 4)
            rows = pl.ds(pl.multiple_of(g * message, 16), message)
            stacked = jnp.concatenate(
                [
                    gather_x[rows, 0:wide], gather_x[rows, wide:width],
                    gather_dy[rows, 0:wide], gather_dy[rows, wide:width],
                ],
                axis=0,
            )
            into = pl.ds(pl.multiple_of((s * plane // 4 + g) * group, 16), group)
            send[into, :] = jnp.dot(
                fold_ref[1], stacked, preferred_element_type=F32
            ).astype(BF)
            for j in range(4):
                start_plane(send, land, s, g * 4 + j, s_xy, r_xy)

    def unfold(s):
        @pl.loop(0, plane // 4)
        def _(g):
            for j in range(4):
                wait_plane(send, land, s, g * 4 + j, s_xy, r_xy)
            here_rows = pl.ds(pl.multiple_of((s * plane // 4 + g) * group, 16), group)
            out = jnp.dot(fold_ref[0], land[here_rows, :], preferred_element_type=F32).astype(BF)
            into = pl.ds(pl.multiple_of((s * plane // 4 + g) * message, 16), message)
            rows_x[into, 0:wide] = out[0:message]
            rows_x[into, wide:width] = out[message : 2 * message]
            rows_dy[into, 0:wide] = out[2 * message : 3 * message]
            rows_dy[into, wide:width] = out[3 * message : 4 * message]

    def own_rows(f, k, which):
        start = lax.div(k, blocks) * side_rows + which * (side_rows // 2) + f * part_rows
        return pl.ds(pl.multiple_of(start, 16), part_rows)

    def buf_rows(f, k):
        start = lax.div(k, blocks) * (side_rows // 2) + f * part_rows
        return pl.ds(pl.multiple_of(start, 16), part_rows)

    def block_of(k):
        return lax.rem(k, blocks)

    def send_sib(f, k):
        return pltpu.make_async_remote_copy(
            src_ref=part.at[block_of(k), own_rows(f, k, 1 - core)],
            dst_ref=from_sib.at[block_of(k), buf_rows(f, k)],
            send_sem=s_sib.at[f, k], recv_sem=r_sib.at[f, k],
            device_id=sib, device_id_type=MESH,
        )

    def send_rs(f, k):
        return pltpu.make_async_remote_copy(
            src_ref=part.at[block_of(k), own_rows(f, k, core)],
            dst_ref=from_prev.at[block_of(k), buf_rows(f, k)],
            send_sem=s_rs.at[f, k], recv_sem=r_rs.at[f, k],
            device_id={"dp": me + 2 if f == 0 else me - 2}, device_id_type=MESH,
        )

    def send_done(f, k, target, sent, got):
        here_done = done.at[block_of(k), own_rows(f, k, core)]
        return pltpu.make_async_remote_copy(
            src_ref=here_done, dst_ref=here_done, send_sem=sent.at[f, k], recv_sem=got.at[f, k],
            device_id=target, device_id_type=MESH,
        )

    def send_ag(f, k):
        return send_done(f, k, {"dp": me - 2 if f == 0 else me + 2}, s_ag, r_ag)

    def send_fin(f, k):
        return send_done(f, k, sib, s_fin, r_fin)

    def parts(side):
        @pl.loop(0, blocks)
        def _(h):
            cols = pl.ds(pl.multiple_of(h * BLOCK, BLOCK), BLOCK)
            for turn in range(2):
                which = 1 - core if turn == 0 else core
                start = pl.multiple_of(side * side_rows + which * (side_rows // 2), 16)
                rows = pl.ds(start, side_rows // 2)
                part[h, rows, 0:BLOCK] = jnp.dot(
                    rows_x[rows, :], wg_ref[:, cols], preferred_element_type=F32
                ).astype(BF)
                part[h, rows, BLOCK : 2 * BLOCK] = jnp.dot(
                    rows_x[rows, :], wu_ref[:, cols], preferred_element_type=F32
                ).astype(BF)
                part[h, rows, 2 * BLOCK : 3 * BLOCK] = dot_last(
                    rows_dy[rows, :], wd_ref[cols, :]
                ).astype(BF)
                if turn == 0:
                    for f in range(2):
                        send_sib(f, side * blocks + h).start()

    def step(tick):
        for f in range(2):
            q = chip if f == 0 else last - chip
            k = tick - q

            @pl.when((k >= 0) & (k < count))
            def _():
                send_sib(f, k).wait_recv()
                mine = own_rows(f, k, core)
                h = block_of(k)
                buf = buf_rows(f, k)

                @pl.when(q == 0)
                def _():
                    part[h, mine, :] = (
                        part[h, mine, :].astype(F32) + from_sib[h, buf, :].astype(F32)
                    ).astype(BF)

                @pl.when(q > 0)
                def _():
                    send_rs(f, k).wait_recv()

                @pl.when((q > 0) & (q < last))
                def _():
                    part[h, mine, :] = (
                        part[h, mine, :].astype(F32)
                        + from_sib[h, buf, :].astype(F32)
                        + from_prev[h, buf, :].astype(F32)
                    ).astype(BF)

                @pl.when(q < last)
                def _():
                    send_rs(f, k).start()

                @pl.when(q == last)
                def _():
                    sums = []
                    for c in range(3):
                        cols = pl.ds(c * BLOCK, BLOCK)
                        sums.append(
                            part[h, mine, cols].astype(F32)
                            + from_sib[h, buf, cols].astype(F32)
                            + from_prev[h, buf, cols].astype(F32)
                        )
                    for c, value in enumerate(swiglu_back(*sums)):
                        done[h, mine, pl.ds(c * BLOCK, BLOCK)] = value
                    send_ag(f, k).start()
                    send_fin(f, k).start()

        for f in range(2):
            q = chip if f == 0 else last - chip
            k = tick - 2 * last + q

            @pl.when((q < last) & (k >= 0) & (k < count))
            def _():
                send_ag(f, k).wait_recv()

                @pl.when(q > 0)
                def _():
                    send_ag(f, k).start()

                send_fin(f, k).start()

    def wait_fin(k):
        for f in range(2):
            send_fin(f, k).wait_recv()

    def send_back(side):
        rows = pl.ds(side * side_rows, side_rows)
        total = None
        for h in range(blocks):
            cols = pl.ds(h * BLOCK, BLOCK)
            term = dot_last(done[h, rows, BLOCK : 2 * BLOCK], wg_ref[:, cols]) + dot_last(
                done[h, rows, 2 * BLOCK : 3 * BLOCK], wu_ref[:, cols]
            )
            total = term if total is None else total + term
        route[...] = total.astype(BF)

        @pl.loop(0, plane // 4)
        def _(g):
            block = pl.ds(pl.multiple_of(g * message, 16), message)
            stacked = jnp.concatenate(
                [route[block, p * thin : (p + 1) * thin] for p in range(4)], axis=0
            )
            into = pl.ds(pl.multiple_of((side * plane // 4 + g) * group, 16), group)
            back_send[into, :] = jnp.dot(
                fold_ref[1], stacked, preferred_element_type=F32
            ).astype(BF)
            for j in range(4):
                start_plane(back_send, back_land, side, g * 4 + j, s_back, r_back)

    def combine(side, info):
        @pl.loop(0, plane // 4)
        def _(g):
            for j in range(4):
                wait_plane(back_send, back_land, side, g * 4 + j, s_back, r_back)
            block = pl.ds(pl.multiple_of((side * plane // 4 + g) * group, 16), group)
            out = jnp.dot(fold_ref[0], back_land[block, :], preferred_element_type=F32).astype(BF)
            into = pl.ds(pl.multiple_of(g * message, 16), message)
            for p in range(4):
                returned[into, p * thin : (p + 1) * thin] = out[p * message : (p + 1) * message]

        codes = row_codes((tok, side_rows), 1)
        hits = None
        for k in range(2):
            hit = codes == column_of(info[k : k + 1, 0:tok]).astype(jnp.int32)
            hits = hit if hits is None else hits | hit
        return jnp.dot(
            jnp.where(hits, 1.0, 0.0).astype(BF), returned[...], preferred_element_type=F32
        )

    dispatch(0, tok_ref, cot_ref, meta)
    meta_copy.wait_recv()
    crossing(0).wait_recv()
    crossing(1).wait_recv()
    dispatch(1, far.at[0], far.at[1], far_meta)

    unfold(0)
    parts(0)
    pl.loop(0, blocks)(step)
    unfold(1)
    parts(1)
    pl.loop(blocks, blocks + 2 * last)(step)

    for k in range(blocks):
        wait_fin(k)
    send_back(0)

    def pair_copy(h):
        rows = pl.ds(pl.multiple_of(h * BLOCK, BLOCK), BLOCK)
        return pltpu.make_async_remote_copy(
            src_ref=pair_send.at[rows], dst_ref=pair_land.at[rows],
            send_sem=s_pair.at[h], recv_sem=r_pair.at[h],
            device_id=pair, device_id_type=MESH,
        )

    @pl.loop(0, blocks)
    def _(h):
        step(h + blocks + 2 * last)
        wait_fin(h + blocks)
        rows = pl.ds(pl.multiple_of(h * BLOCK, BLOCK), BLOCK)
        own[rows, :] = dot_first(done[h, :, 0:BLOCK], rows_dy[...])
        pair_send[rows, :] = own[rows, :].astype(BF)
        pair_copy(h).start()

    send_back(1)

    cross = pltpu.make_async_remote_copy(
        src_ref=cross_send, dst_ref=cross_land, send_sem=s_cross, recv_sem=r_cross,
        device_id=across, device_id_type=MESH,
    )
    partial[...] = combine(0, meta)
    cross_send[...] = combine(1, far_meta).astype(BF)
    cross.start()

    hot = jnp.max(
        jnp.where(hot_ref[...] == lax.rem(spot, plane), 1.0, 0.0), axis=1, keepdims=True
    )

    @pl.loop(0, blocks)
    def _(h):
        pair_copy(h).wait_recv()
        rows = pl.ds(pl.multiple_of(h * BLOCK, BLOCK), BLOCK)
        grad_down_ref[rows, :] = (own[rows, :] + hot * pair_land[rows, :].astype(F32)).astype(BF)

    cross.wait_recv()
    grad_tok_ref[...] = (partial[...] + cross_land[...].astype(F32)).astype(BF)

    meta_copy.wait_send()
    cross.wait_send()
    for d in range(2):
        crossing(d).wait_send()

    @pl.loop(1, plane)
    def _(hop):
        there = lax.rem(here + hop, plane)
        for s in range(2):
            to_plane(send, land, s, there, s_xy, r_xy).wait_send()
            to_plane(back_send, back_land, s, there, s_back, r_back).wait_send()

    @pl.loop(0, count)
    def _(k):
        for f in range(2):
            q = chip if f == 0 else last - chip
            send_sib(f, k).wait_send()
            send_fin(f, k).wait_send()

            @pl.when(q < last)
            def _():
                send_rs(f, k).wait_send()

            @pl.when(q > 0)
            def _():
                send_ag(f, k).wait_send()

    @pl.loop(0, blocks)
    def _(h):
        pair_copy(h).wait_send()


def fold_orders():
    order = np.arange(16 * CAP).reshape(4, 4, CAP).transpose(1, 0, 2).reshape(-1)
    unfold = np.eye(16 * CAP, dtype=np.float32)[order]
    return np.stack([unfold, unfold.T])


def on_device(
    tokens, cotangent, gate_scale, expert_ids, expert_slots, hot_pairs, w_gate, w_up, w_down
):
    tok, width = tokens.shape
    hid = w_gate.shape[2]
    plane = NX * NY
    side_rows = plane * CAP
    rows = 2 * side_rows
    message = 4 * CAP
    blocks = hid // BLOCK
    count = 2 * blocks
    dma = pltpu.SemaphoreType.DMA
    flow = [dma((2, count))] * 8
    grad_tokens, grad_down = pl.pallas_call(
        layer_kernel,
        out_shape=(
            jax.ShapeDtypeStruct((tok, width), BF),
            jax.ShapeDtypeStruct((hid, width), BF),
        ),
        in_specs=[pl.BlockSpec(memory_space=pltpu.VMEM)] * 10,
        out_specs=[pl.BlockSpec(memory_space=pltpu.VMEM)] * 2,
        scratch_shapes=[
            pltpu.VMEM((2, tok, width), BF),
            pltpu.VMEM((8, 256), F32),
            pltpu.VMEM((8, 256), F32),
            pltpu.VMEM((side_rows, width), BF),
            pltpu.VMEM((side_rows, width), BF),
            pltpu.VMEM((2 * plane * message, width // 2), BF),
            pltpu.VMEM((2 * plane * message, width // 2), BF),
            pltpu.VMEM((rows, width), BF),
            pltpu.VMEM((rows, width), BF),
            pltpu.VMEM((blocks, rows, 3 * BLOCK), BF),
            pltpu.VMEM((blocks, side_rows, 3 * BLOCK), BF),
            pltpu.VMEM((blocks, side_rows, 3 * BLOCK), BF),
            pltpu.VMEM((blocks, rows, 3 * BLOCK), BF),
            pltpu.VMEM((side_rows, width), BF),
            pltpu.VMEM((2 * plane * message, width // 4), BF),
            pltpu.VMEM((2 * plane * message, width // 4), BF),
            pltpu.VMEM((side_rows, width), BF),
            pltpu.VMEM((tok, width), F32),
            pltpu.VMEM((tok, width), BF),
            pltpu.VMEM((tok, width), BF),
            pltpu.VMEM((hid, width), F32),
            pltpu.VMEM((hid, width), BF),
            pltpu.VMEM((hid, width), BF),
            dma((2,)), dma((2,)), dma, dma, dma((2, plane)), dma((2, plane)),
        ] + flow + [
            dma((2, plane)), dma((2, plane)), dma, dma, dma((blocks,)), dma((blocks,)),
        ],
        compiler_params=pltpu.CompilerParams(
            collective_id=0, has_side_effects=True, vmem_limit_bytes=52 * 1024 * 1024
        ),
        cost_estimate=pl.CostEstimate(
            flops=12 * rows * width * hid, bytes_accessed=8 * 1024 * 1024, transcendentals=0
        ),
        name="layer_backward",
    )(
        tokens, cotangent, gate_scale.T, expert_ids.T, expert_slots, hot_pairs.reshape(1, -1),
        jnp.asarray(fold_orders(), dtype=BF), w_gate[0], w_up[0], w_down[0],
    )
    return grad_tokens, grad_down[None]


def solution(mesh):
    placed = (
        P("expert", "dp"),
        P("expert", "dp"),
        P("expert", None),
        P("expert", None),
        P(),
        P(),
        P("expert", "dp", None),
        P("expert", "dp", None),
        P("expert", None, "dp"),
    )
    return jax.shard_map(
        on_device,
        mesh=mesh,
        in_specs=placed,
        out_specs=(P("expert", "dp"), P("expert", None, "dp")),
        check_vma=False,
    )
```

time: 304 us -> 160 us (0.53)
  waiting for transfers between devices: 201 us -> 0 us
  Pallas kernels: 0 us -> 153 us
  starting transfers between devices: 47.4 us -> 0 us
  matrix products: 24 us -> 0 us
  between operations: 14.9 us -> 0.65 us
  other arithmetic: 5.66 us -> 0 us
  local copies, waits for them, and re-layouts: 10.6 us -> 5.8 us
    pallas_call x0 -> x1, Pallas kernels: none -> 153 us  [on_device(): pl.pallas_call(layer_kernel, out_shape=(jax.ShapeDtypeStruct((tok, width)...]
    psum x1 -> x0, waiting for transfers between devices: 124 us -> none  [on_device(): lax.psum(up_part.astype(jnp.bfloat16), 'dp').astype(jnp.float32)]
    all_to_all x3 -> x0, waiting for transfers between devices: 46.8 us -> none  [the longest x1 25.2 us: on_device(): lax.all_to_all(send_x, 'expert', split_axis=0, concat_axis=0, tiled=True)]
    all_to_all x3 -> x0, starting transfers between devices: 42.8 us -> none  [the longest x1 19.7 us: on_device(): lax.all_to_all(send_x, 'expert', split_axis=0, concat_axis=0, tiled=True)]
    ppermute x1 -> x0, waiting for transfers between devices: 30.2 us -> none  [from_partner(): return lax.ppermute(block, axis, route)]
    dot_general x9 -> x0, matrix products: 24 us -> none  [the longest x3 9.02 us: contract_last(): lax.dot_general(left, right, (((1,), (1,)), ((), ())), preferred_element_...]
    unnamed x23 -> x17, local copies, waits for them, and re-layouts: 0.17 us -> 5.8 us
    reshape x8 -> x0, local copies, waits for them, and re-layouts: 5.13 us -> none  [the longest x1 1.15 us: on_device(): route_grad.reshape(slot_count, capacity, width)]
  transfers between devices with their start and end apart: 5 -> 0, of which waited for: 4 -> 0; matrix products, arithmetic and copies ran while one was open for 7% -> 0% of each run, Pallas kernels for 0% -> 0%
where the time goes in v3:
time: 160 us
  Pallas kernels  153 us (96%)
  local copies, waits for them, and re-layouts  5.8 us (4%)
    pallas_call x1, Pallas kernels, on_device(): pl.pallas_call(layer_kernel, out_shape=(jax.ShapeDtypeStruct((tok, width)...  153 us
    unnamed x17, local copies, waits for them, and re-layouts  5.8 us

profile of v3, /device:TPU:1, one launch (start us, length us, event | category | flops | bytes accessed | tf_op | source)
XLA Modules:
  0.0 159.8 jit_solution(7645198656897630737)
XLA Ops:
  0.6 0.0 copy-start.6
  0.6 0.7 copy-done.6
  1.3 0.0 copy-start.2
  1.3 0.0 copy-start.3
  1.3 0.0 copy-start.4
  1.3 0.1 copy.12.slots_ref
  1.4 0.6 copy-done.2
  2.0 0.0 copy-done.3
  2.0 0.0 copy-done.4
  2.0 0.0 copy-start
  2.0 0.9 copy-done
  2.9 0.0 copy-start.1
  2.9 0.9 copy-done.1
  3.9 0.0 copy-start.5
  3.9 0.9 copy-done.5
  4.8 153.4 %layer_backward.1 = (bf16[192,512]{1,0:T(8,128)(2,1)S(1)}, bf16[1024,512]{1,0:T(8,128)(2,1)S(1)}) custom-call(bf16[192,512]{1,0:T(8,128)(2,1)S(1)} %copy-done, bf16[192,512]{1,0:T(8,128)(2,1)S(1)} %copy-done.1, f32[2,192]{1,0:T(2,128)S(1)} %bitcast.8, s32[2,192]{1,0:T(2,128)S(1)} %bitcast.9, s32[48,2]{1,0:T(8,128)S(1)} %copy.12.slots_ref, ...), custom_call_target="tpu_custom_call" | custom-call | flops 4831838208 | bytes 8388608 | tf_op jit(solution)/shard_map/layer_backward/pallas_call | solution.py:558
  158.2 0.7 copy.15
  158.8 1.0 copy.16
Async XLA Ops:
  0.6 0.7 copy-start.6
  1.3 0.7 copy-start.2
  1.3 0.7 copy-start.3
  1.3 0.7 copy-start.4
  2.0 0.9 copy-start
  2.9 0.9 copy-start.1
  3.9 0.9 copy-start.5

commit v4 on v3

--- a/solution.py
+++ b/solution.py
@@ -13,6 +13,7 @@
 NX = 4
 NY = 8
 BLOCK = 256
+LAG = 2
 
 
 def swiglu_back(gate_sum, up_sum, grad_hidden):
@@ -81,16 +82,17 @@
 
 def route_targets(ids_ref, slots_ref, slot_count, capacity):
     tok = ids_ref.shape[1]
-    experts = slots_ref.shape[0]
+    experts = slots_ref.shape[1]
     odd = lax.broadcasted_iota(jnp.int32, (experts, tok), 1) % 2 == 1
-    table = jnp.where(odd, slots_ref[:, 1:2], slots_ref[:, 0:1])
+    first, second = [column_of(slots_ref[k : k + 1, :].astype(F32)) for k in range(2)]
+    table = jnp.where(odd, second, first)
     expert_row = lax.broadcasted_iota(jnp.int32, (experts, tok), 0)
     slot_row = lax.broadcasted_iota(jnp.int32, (slot_count, tok), 0)
     slots = [
-        jnp.sum(jnp.where(ids_ref[k : k + 1, :] == expert_row, table, 0), axis=0, keepdims=True)
+        jnp.sum(jnp.where(ids_ref[k : k + 1, :] == expert_row, table, 0.0), axis=0, keepdims=True)
         for k in range(2)
     ]
-    hits = [jnp.where(slot == slot_row, 1.0, 0.0) for slot in slots]
+    hits = [jnp.where(slot.astype(jnp.int32) == slot_row, 1.0, 0.0) for slot in slots]
     earlier = lax.broadcasted_iota(jnp.int32, (tok, tok), 0) < lax.broadcasted_iota(
         jnp.int32, (tok, tok), 1
     )
@@ -100,19 +102,20 @@
         preferred_element_type=F32,
     )
     return [
-        slot.astype(F32) * capacity + jnp.sum(hit * before, axis=0, keepdims=True)
+        slot * capacity + jnp.sum(hit * before, axis=0, keepdims=True)
         for slot, hit in zip(slots, hits)
     ]
 
 
 def layer_kernel(
-    tok_ref, cot_ref, scale_ref, ids_ref, slots_ref, hot_ref, fold_ref, wg_ref, wu_ref, wd_ref,
+    tok_any, cot_any, scale_any, ids_any, slots_any, hot_any, fold_any, wg_any, wu_any, wd_any,
     grad_tok_ref, grad_down_ref,
+    ids_ref, slots_ref, scale_ref, tok_ref, cot_ref, fold_ref, hot_ref, wg_ref, wu_ref, wd_ref,
     far, meta, far_meta, gather_x, gather_dy, send, land, rows_x, rows_dy,
     part, from_sib, from_prev, done, route, back_send, back_land, returned,
-    partial, cross_send, cross_land, own, pair_send, pair_land,
+    partial, cross_send, cross_land, own, hid_send, pair_hid, pair_dy,
     s_z, r_z, s_meta, r_meta, s_xy, r_xy, s_sib, r_sib, s_rs, r_rs, s_ag, r_ag, s_fin, r_fin,
-    s_back, r_back, s_cross, r_cross, s_pair, r_pair,
+    s_back, r_back, s_cross, r_cross, s_pair, r_pair, s_pdy, r_pdy, s_half, r_half, s_load,
 ):
     tok, width = tok_ref.shape
     hid = wg_ref.shape[1]
@@ -122,8 +125,9 @@
     message = 4 * CAP
     group = 4 * message
     wide, thin = width // 2, width // 4
-    part_rows = side_rows // 4
-    count = 2 * blocks
+    stage_rows = side_rows // 2
+    part_rows = stage_rows // 4
+    count = 4 * blocks
     x, z_hi, y, z, core = coords()
     here = x * NY + y
     spot = lax.axis_index("expert")
@@ -135,6 +139,17 @@
     pair = {"expert": lax.rem(spot + plane, 2 * plane)}
     inner = (chip > 0) & (chip < last)
 
+    held = [
+        (ids_any, ids_ref), (slots_any, slots_ref), (scale_any, scale_ref), (tok_any, tok_ref),
+        (cot_any, cot_ref), (fold_any, fold_ref), (hot_any, hot_ref),
+        (wg_any, wg_ref), (wu_any, wu_ref), (wd_any, wd_ref),
+    ]
+    loads = [
+        pltpu.make_async_copy(there, kept, s_load.at[i]) for i, (there, kept) in enumerate(held)
+    ]
+    for load in loads:
+        load.start()
+
     barrier = pltpu.get_barrier_semaphore()
     signal_all(barrier, (across, sib))
     signal_plane(barrier, x, z_hi, y)
@@ -147,6 +162,8 @@
     def _():
         signal_all(barrier, ({"dp": me + 2},))
 
+    for load in loads[:3]:
+        load.wait()
     targets = route_targets(ids_ref, slots_ref, 2 * plane, CAP)
     meta[...] = jnp.zeros_like(meta)
     for k in range(2):
@@ -162,7 +179,7 @@
         pl.semaphore_wait(barrier, plane + 2)
 
     def crossing(d):
-        source = tok_ref if d == 0 else cot_ref
+        source = tok_any if d == 0 else cot_any
         return pltpu.make_async_remote_copy(
             src_ref=source, dst_ref=far.at[d], send_sem=s_z.at[d], recv_sem=r_z.at[d],
             device_id=across, device_id_type=MESH,
@@ -246,7 +263,7 @@
 
         @pl.loop(0, plane // 4)
         def _(step):
-            g = lax.rem(step + 2 * x + plane // 8, plane // 4)
+            g = lax.rem(step + 2 * x, plane // 4)
             rows = pl.ds(pl.multiple_of(g * message, 16), message)
             stacked = jnp.concatenate(
                 [
@@ -262,25 +279,33 @@
             for j in range(4):
                 start_plane(send, land, s, g * 4 + j, s_xy, r_xy)
 
-    def unfold(s):
-        @pl.loop(0, plane // 4)
-        def _(g):
+    def group_at(spot_at):
+        column = lax.rem(x + NX - lax.div(spot_at, 2), NX)
+        return column * 2 + lax.rem(spot_at, 2)
+
+    def unfold(stage):
+        s = stage // 2
+
+        @pl.loop(0, plane // 8)
+        def _(i):
+            spot_at = (stage % 2) * (plane // 8) + i
+            g = group_at(spot_at)
             for j in range(4):
                 wait_plane(send, land, s, g * 4 + j, s_xy, r_xy)
             here_rows = pl.ds(pl.multiple_of((s * plane // 4 + g) * group, 16), group)
             out = jnp.dot(fold_ref[0], land[here_rows, :], preferred_element_type=F32).astype(BF)
-            into = pl.ds(pl.multiple_of((s * plane // 4 + g) * message, 16), message)
+            into = pl.ds(pl.multiple_of((s * plane // 4 + spot_at) * message, 16), message)
             rows_x[into, 0:wide] = out[0:message]
             rows_x[into, wide:width] = out[message : 2 * message]
             rows_dy[into, 0:wide] = out[2 * message : 3 * message]
             rows_dy[into, wide:width] = out[3 * message : 4 * message]
 
     def own_rows(f, k, which):
-        start = lax.div(k, blocks) * side_rows + which * (side_rows // 2) + f * part_rows
+        start = lax.div(k, blocks) * stage_rows + which * (stage_rows // 2) + f * part_rows
         return pl.ds(pl.multiple_of(start, 16), part_rows)
 
     def buf_rows(f, k):
-        start = lax.div(k, blocks) * (side_rows // 2) + f * part_rows
+        start = lax.div(k, blocks) * (stage_rows // 2) + f * part_rows
         return pl.ds(pl.multiple_of(start, 16), part_rows)
 
     def block_of(k):
@@ -315,31 +340,23 @@
     def send_fin(f, k):
         return send_done(f, k, sib, s_fin, r_fin)
 
-    def parts(side):
-        @pl.loop(0, blocks)
-        def _(h):
-            cols = pl.ds(pl.multiple_of(h * BLOCK, BLOCK), BLOCK)
-            for turn in range(2):
-                which = 1 - core if turn == 0 else core
-                start = pl.multiple_of(side * side_rows + which * (side_rows // 2), 16)
-                rows = pl.ds(start, side_rows // 2)
-                part[h, rows, 0:BLOCK] = jnp.dot(
-                    rows_x[rows, :], wg_ref[:, cols], preferred_element_type=F32
-                ).astype(BF)
-                part[h, rows, BLOCK : 2 * BLOCK] = jnp.dot(
-                    rows_x[rows, :], wu_ref[:, cols], preferred_element_type=F32
-                ).astype(BF)
-                part[h, rows, 2 * BLOCK : 3 * BLOCK] = dot_last(
-                    rows_dy[rows, :], wd_ref[cols, :]
-                ).astype(BF)
-                if turn == 0:
-                    for f in range(2):
-                        send_sib(f, side * blocks + h).start()
+    def parts(stage, h):
+        rows = pl.ds(stage * stage_rows, stage_rows)
+        cols = pl.ds(pl.multiple_of(h * BLOCK, BLOCK), BLOCK)
+        part[h, rows, 0:BLOCK] = jnp.dot(
+            rows_x[rows, :], wg_ref[:, cols], preferred_element_type=F32
+        ).astype(BF)
+        part[h, rows, BLOCK : 2 * BLOCK] = jnp.dot(
+            rows_x[rows, :], wu_ref[:, cols], preferred_element_type=F32
+        ).astype(BF)
+        part[h, rows, 2 * BLOCK : 3 * BLOCK] = dot_last(rows_dy[rows, :], wd_ref[cols, :]).astype(BF)
+        for f in range(2):
+            send_sib(f, stage * blocks + h).start()
 
     def step(tick):
         for f in range(2):
             q = chip if f == 0 else last - chip
-            k = tick - q
+            k = tick - 1 - LAG * q
 
             @pl.when((k >= 0) & (k < count))
             def _():
@@ -387,7 +404,7 @@
 
         for f in range(2):
             q = chip if f == 0 else last - chip
-            k = tick - 2 * last + q
+            k = tick - 1 - LAG * (2 * last - q)
 
             @pl.when((q < last) & (k >= 0) & (k < count))
             def _():
@@ -403,8 +420,9 @@
         for f in range(2):
             send_fin(f, k).wait_recv()
 
-    def send_back(side):
-        rows = pl.ds(side * side_rows, side_rows)
+    def send_back(stage):
+        side = stage // 2
+        rows = pl.ds(stage * stage_rows, stage_rows)
         total = None
         for h in range(blocks):
             cols = pl.ds(h * BLOCK, BLOCK)
@@ -414,9 +432,10 @@
             total = term if total is None else total + term
         route[...] = total.astype(BF)
 
-        @pl.loop(0, plane // 4)
-        def _(g):
-            block = pl.ds(pl.multiple_of(g * message, 16), message)
+        @pl.loop(0, plane // 8)
+        def _(i):
+            g = group_at((stage % 2) * (plane // 8) + i)
+            block = pl.ds(pl.multiple_of(i * message, 16), message)
             stacked = jnp.concatenate(
                 [route[block, p * thin : (p + 1) * thin] for p in range(4)], axis=0
             )
@@ -447,47 +466,99 @@
             jnp.where(hits, 1.0, 0.0).astype(BF), returned[...], preferred_element_type=F32
         )
 
+    for load in loads[3:7]:
+        load.wait()
     dispatch(0, tok_ref, cot_ref, meta)
     meta_copy.wait_recv()
     crossing(0).wait_recv()
     crossing(1).wait_recv()
     dispatch(1, far.at[0], far.at[1], far_meta)
 
-    unfold(0)
-    parts(0)
-    pl.loop(0, blocks)(step)
-    unfold(1)
-    parts(1)
-    pl.loop(blocks, blocks + 2 * last)(step)
-
-    for k in range(blocks):
-        wait_fin(k)
-    send_back(0)
-
-    def pair_copy(h):
-        rows = pl.ds(pl.multiple_of(h * BLOCK, BLOCK), BLOCK)
-        return pltpu.make_async_remote_copy(
-            src_ref=pair_send.at[rows], dst_ref=pair_land.at[rows],
-            send_sem=s_pair.at[h], recv_sem=r_pair.at[h],
+    def pair_dy_copy(stage):
+        rows = pl.ds(stage * stage_rows, stage_rows)
+        return pltpu.make_async_remote_copy(
+            src_ref=rows_dy.at[rows], dst_ref=pair_dy.at[rows],
+            send_sem=s_pdy.at[stage], recv_sem=r_pdy.at[stage],
             device_id=pair, device_id_type=MESH,
         )
+
+    half_rows = stage_rows // 2
+
+    def core_half(stage):
+        return pl.ds(pl.multiple_of(stage * stage_rows + core * half_rows, 16), half_rows)
+
+    def pair_hid_copy(stage):
+        return pltpu.make_async_remote_copy(
+            src_ref=hid_send.at[pl.ds(stage * half_rows, half_rows)],
+            dst_ref=pair_hid.at[core_half(stage)],
+            send_sem=s_pair.at[stage], recv_sem=r_pair.at[stage],
+            device_id=pair, device_id_type=MESH,
+        )
+
+    def share_half(stage):
+        return pltpu.make_async_remote_copy(
+            src_ref=pair_hid.at[core_half(stage)], dst_ref=pair_hid.at[core_half(stage)],
+            send_sem=s_half.at[stage], recv_sem=r_half.at[stage],
+            device_id=sib, device_id_type=MESH,
+        )
+
+    def send_hidden(stage):
+        for h in range(blocks):
+            hid_send[pl.ds(stage * half_rows, half_rows), pl.ds(h * BLOCK, BLOCK)] = done[
+                h, core_half(stage), 0:BLOCK
+            ]
+        pair_hid_copy(stage).start()
+
+    def pass_on(stage):
+        pair_hid_copy(stage).wait_recv()
+        share_half(stage).start()
+
+    for load in loads[7:]:
+        load.wait()
+    drain = 1 + 2 * LAG * last
+    stages = count // blocks
+
+    def finish(stage):
+        for h in range(blocks):
+            wait_fin(stage * blocks + h)
+        send_hidden(stage)
+        send_back(stage)
+        if stage > 0:
+            pass_on(stage - 1)
+
+    finished = 0
+    tick = 0
+    for stage in range(stages):
+        unfold(stage)
+        pair_dy_copy(stage).start()
+
+        @pl.loop(0, blocks)
+        def _(h):
+            parts(stage, h)
+            step(stage * blocks + h)
+
+        tick += blocks
+    while finished < stages - 1:
+        stop = (finished + 1) * blocks + drain
+        pl.loop(tick, stop)(step)
+        tick = stop
+        finish(finished)
+        finished += 1
+
+    pl.loop(tick, tick + blocks)(step)
+    finish(stages - 1)
 
     @pl.loop(0, blocks)
     def _(h):
-        step(h + blocks + 2 * last)
-        wait_fin(h + blocks)
         rows = pl.ds(pl.multiple_of(h * BLOCK, BLOCK), BLOCK)
         own[rows, :] = dot_first(done[h, :, 0:BLOCK], rows_dy[...])
-        pair_send[rows, :] = own[rows, :].astype(BF)
-        pair_copy(h).start()
-
-    send_back(1)
 
     cross = pltpu.make_async_remote_copy(
         src_ref=cross_send, dst_ref=cross_land, send_sem=s_cross, recv_sem=r_cross,
         device_id=across, device_id_type=MESH,
     )
     partial[...] = combine(0, meta)
+    pass_on(stages - 1)
     cross_send[...] = combine(1, far_meta).astype(BF)
     cross.start()
 
@@ -495,11 +566,15 @@
         jnp.where(hot_ref[...] == lax.rem(spot, plane), 1.0, 0.0), axis=1, keepdims=True
     )
 
+    for stage in range(stages):
+        pair_dy_copy(stage).wait_recv()
+        share_half(stage).wait_recv()
+
     @pl.loop(0, blocks)
     def _(h):
-        pair_copy(h).wait_recv()
         rows = pl.ds(pl.multiple_of(h * BLOCK, BLOCK), BLOCK)
-        grad_down_ref[rows, :] = (own[rows, :] + hot * pair_land[rows, :].astype(F32)).astype(BF)
+        theirs = dot_first(pair_hid[:, rows], pair_dy[...])
+        grad_down_ref[rows, :] = (own[rows, :] + hot * theirs).astype(BF)
 
     cross.wait_recv()
     grad_tok_ref[...] = (partial[...] + cross_land[...].astype(F32)).astype(BF)
@@ -531,9 +606,10 @@
             def _():
                 send_ag(f, k).wait_send()
 
-    @pl.loop(0, blocks)
-    def _(h):
-        pair_copy(h).wait_send()
+    for stage in range(stages):
+        pair_dy_copy(stage).wait_send()
+        pair_hid_copy(stage).wait_send()
+        share_half(stage).wait_send()
 
 
 def fold_orders():
@@ -552,7 +628,7 @@
     rows = 2 * side_rows
     message = 4 * CAP
     blocks = hid // BLOCK
-    count = 2 * blocks
+    count = 4 * blocks
     dma = pltpu.SemaphoreType.DMA
     flow = [dma((2, count))] * 8
     grad_tokens, grad_down = pl.pallas_call(
@@ -561,9 +637,19 @@
             jax.ShapeDtypeStruct((tok, width), BF),
             jax.ShapeDtypeStruct((hid, width), BF),
         ),
-        in_specs=[pl.BlockSpec(memory_space=pltpu.VMEM)] * 10,
+        in_specs=[pl.BlockSpec(memory_space=pl.ANY)] * 10,
         out_specs=[pl.BlockSpec(memory_space=pltpu.VMEM)] * 2,
         scratch_shapes=[
+            pltpu.VMEM(expert_ids.shape[::-1], jnp.int32),
+            pltpu.VMEM(expert_slots.shape[::-1], jnp.int32),
+            pltpu.VMEM(gate_scale.shape[::-1], F32),
+            pltpu.VMEM((tok, width), BF),
+            pltpu.VMEM((tok, width), BF),
+            pltpu.VMEM((2, 16 * CAP, 16 * CAP), BF),
+            pltpu.VMEM((1, hot_pairs.shape[0]), jnp.int32),
+            pltpu.VMEM((width, hid), BF),
+            pltpu.VMEM((width, hid), BF),
+            pltpu.VMEM((hid, width), BF),
             pltpu.VMEM((2, tok, width), BF),
             pltpu.VMEM((8, 256), F32),
             pltpu.VMEM((8, 256), F32),
@@ -577,7 +663,7 @@
             pltpu.VMEM((blocks, side_rows, 3 * BLOCK), BF),
             pltpu.VMEM((blocks, side_rows, 3 * BLOCK), BF),
             pltpu.VMEM((blocks, rows, 3 * BLOCK), BF),
-            pltpu.VMEM((side_rows, width), BF),
+            pltpu.VMEM((side_rows // 2, width), BF),
             pltpu.VMEM((2 * plane * message, width // 4), BF),
             pltpu.VMEM((2 * plane * message, width // 4), BF),
             pltpu.VMEM((side_rows, width), BF),
@@ -585,11 +671,13 @@
             pltpu.VMEM((tok, width), BF),
             pltpu.VMEM((tok, width), BF),
             pltpu.VMEM((hid, width), F32),
-            pltpu.VMEM((hid, width), BF),
-            pltpu.VMEM((hid, width), BF),
+            pltpu.VMEM((side_rows, hid), BF),
+            pltpu.VMEM((rows, hid), BF),
+            pltpu.VMEM((rows, width), BF),
             dma((2,)), dma((2,)), dma, dma, dma((2, plane)), dma((2, plane)),
         ] + flow + [
-            dma((2, plane)), dma((2, plane)), dma, dma, dma((blocks,)), dma((blocks,)),
+            dma((2, plane)), dma((2, plane)), dma, dma, dma((4,)), dma((4,)),
+            dma((4,)), dma((4,)), dma((4,)), dma((4,)), dma((10,)),
         ],
         compiler_params=pltpu.CompilerParams(
             collective_id=0, has_side_effects=True, vmem_limit_bytes=52 * 1024 * 1024
@@ -599,7 +687,7 @@
         ),
         name="layer_backward",
     )(
-        tokens, cotangent, gate_scale.T, expert_ids.T, expert_slots, hot_pairs.reshape(1, -1),
+        tokens, cotangent, gate_scale.T, expert_ids.T, expert_slots.T, hot_pairs.reshape(1, -1),
         jnp.asarray(fold_orders(), dtype=BF), w_gate[0], w_up[0], w_down[0],
     )
     return grad_tokens, grad_down[None]

time: 160 us -> 138 us (0.86)
  Pallas kernels: 153 us -> 132 us
    pallas_call x1, Pallas kernels: 153 us -> 132 us  [on_device(): pl.pallas_call(layer_kernel, out_shape=(jax.ShapeDtypeStruct((tok, width)...]
    unnamed x17 -> x16, local copies, waits for them, and re-layouts: 5.8 us -> 5.11 us
where the time goes in v4:
time: 138 us; the launch traced here: 137 us
  Pallas kernels  132 us (96%)
  local copies, waits for them, and re-layouts  5.11 us (4%)
    pallas_call x1, Pallas kernels, on_device(): pl.pallas_call(layer_kernel, out_shape=(jax.ShapeDtypeStruct((tok, width)...  132 us
    unnamed x16, local copies, waits for them, and re-layouts  5.11 us

profile of v4, /device:TPU:1, one launch (start us, length us, event | category | flops | bytes accessed | tf_op | source)
XLA Modules:
  0.0 137.4 jit_solution(8715869775640746496)
XLA Ops:
  0.6 0.0 copy-start.3
  0.6 0.0 copy-start.2
  0.7 0.0 copy-start.4
  0.7 0.0 copy-start.5
  0.7 0.6 copy-done.3
  1.3 0.0 copy-done.2
  1.3 0.0 copy-done.4
  1.3 0.0 copy-done.5
  1.3 0.0 copy-start
  1.3 0.9 copy-done
  2.3 0.0 copy-start.1
  2.3 0.9 copy-done.1
  3.2 0.0 copy-start.6
  3.2 0.9 copy-done.6
  4.1 131.6 %layer_backward.1 = (bf16[192,512]{1,0:T(8,128)(2,1)S(1)}, bf16[1024,512]{1,0:T(8,128)(2,1)S(1)}) custom-call(bf16[192,512]{1,0:T(8,128)(2,1)S(1)} %copy-done, bf16[192,512]{1,0:T(8,128)(2,1)S(1)} %copy-done.1, f32[2,192]{1,0:T(2,128)S(1)} %bitcast.9, s32[2,192]{1,0:T(2,128)S(1)} %bitcast.10, s32[2,48]{1,0:T(2,128)S(1)} %bitcast.11, s32[1,16]{1,0:T(1,128)S(1)} %bitcast.12, ...), custom_call_target="tpu_custom_call" | custom-call | flops 4831838208 | bytes 8388608 | tf_op jit(solution)/shard_map/layer_backward/pallas_call | solution.py:634
  135.8 0.7 copy.14
  136.4 1.0 copy.15
Async XLA Ops:
  0.6 0.7 copy-start.3
  0.6 0.7 copy-start.2
  0.7 0.7 copy-start.4
  0.7 0.7 copy-start.5
  1.3 0.9 copy-start
  2.3 0.9 copy-start.1
  3.2 0.9 copy-start.6

commit v5 on v4

--- a/solution.py
+++ b/solution.py
@@ -1,6 +1,5 @@
 import jax
 import jax.numpy as jnp
-import numpy as np
 from jax import lax
 from jax.experimental import pallas as pl
 from jax.experimental.pallas import tpu as pltpu
@@ -107,10 +106,25 @@
     ]
 
 
+def fold_matrices(fold_ref):
+    size = fold_ref.shape[1]
+    message = size // 4
+    both = []
+    for axis in range(2):
+        row = lax.broadcasted_iota(jnp.int32, (size, size), axis)
+        outer = sum(jnp.where(row >= e * message, 1, 0) for e in range(1, 4))
+        rest = row - outer * message
+        inner = sum(jnp.where(rest >= e * CAP, 1, 0) for e in range(1, 4))
+        both.append(inner * message + outer * CAP + rest - inner * CAP)
+    other = [lax.broadcasted_iota(jnp.int32, (size, size), 1 - axis) for axis in range(2)]
+    for axis in range(2):
+        fold_ref[axis, :, :] = jnp.where(both[axis] == other[axis], 1.0, 0.0).astype(BF)
+
+
 def layer_kernel(
-    tok_any, cot_any, scale_any, ids_any, slots_any, hot_any, fold_any, wg_any, wu_any, wd_any,
+    tok_any, cot_any, scale_any, ids_any, slots_any, hot_any, wg_any, wu_any, wd_any,
     grad_tok_ref, grad_down_ref,
-    ids_ref, slots_ref, scale_ref, tok_ref, cot_ref, fold_ref, hot_ref, wg_ref, wu_ref, wd_ref,
+    ids_ref, slots_ref, scale_ref, tok_ref, cot_ref, hot_ref, fold_ref, wg_ref, wu_ref, wd_ref,
     far, meta, far_meta, gather_x, gather_dy, send, land, rows_x, rows_dy,
     part, from_sib, from_prev, done, route, back_send, back_land, returned,
     partial, cross_send, cross_land, own, hid_send, pair_hid, pair_dy,
@@ -141,7 +155,7 @@
 
     held = [
         (ids_any, ids_ref), (slots_any, slots_ref), (scale_any, scale_ref), (tok_any, tok_ref),
-        (cot_any, cot_ref), (fold_any, fold_ref), (hot_any, hot_ref),
+        (cot_any, cot_ref), (hot_any, hot_ref),
         (wg_any, wg_ref), (wu_any, wu_ref), (wd_any, wd_ref),
     ]
     loads = [
@@ -162,6 +176,7 @@
     def _():
         signal_all(barrier, ({"dp": me + 2},))
 
+    fold_matrices(fold_ref)
     for load in loads[:3]:
         load.wait()
     targets = route_targets(ids_ref, slots_ref, 2 * plane, CAP)
@@ -466,7 +481,7 @@
             jnp.where(hits, 1.0, 0.0).astype(BF), returned[...], preferred_element_type=F32
         )
 
-    for load in loads[3:7]:
+    for load in loads[3:6]:
         load.wait()
     dispatch(0, tok_ref, cot_ref, meta)
     meta_copy.wait_recv()
@@ -513,7 +528,7 @@
         pair_hid_copy(stage).wait_recv()
         share_half(stage).start()
 
-    for load in loads[7:]:
+    for load in loads[6:]:
         load.wait()
     drain = 1 + 2 * LAG * last
     stages = count // blocks
@@ -559,28 +574,7 @@
     )
     partial[...] = combine(0, meta)
     pass_on(stages - 1)
-    cross_send[...] = combine(1, far_meta).astype(BF)
-    cross.start()
-
-    hot = jnp.max(
-        jnp.where(hot_ref[...] == lax.rem(spot, plane), 1.0, 0.0), axis=1, keepdims=True
-    )
-
-    for stage in range(stages):
-        pair_dy_copy(stage).wait_recv()
-        share_half(stage).wait_recv()
-
-    @pl.loop(0, blocks)
-    def _(h):
-        rows = pl.ds(pl.multiple_of(h * BLOCK, BLOCK), BLOCK)
-        theirs = dot_first(pair_hid[:, rows], pair_dy[...])
-        grad_down_ref[rows, :] = (own[rows, :] + hot * theirs).astype(BF)
-
-    cross.wait_recv()
-    grad_tok_ref[...] = (partial[...] + cross_land[...].astype(F32)).astype(BF)
-
     meta_copy.wait_send()
-    cross.wait_send()
     for d in range(2):
         crossing(d).wait_send()
 
@@ -589,7 +583,7 @@
         there = lax.rem(here + hop, plane)
         for s in range(2):
             to_plane(send, land, s, there, s_xy, r_xy).wait_send()
-            to_plane(back_send, back_land, s, there, s_back, r_back).wait_send()
+        to_plane(back_send, back_land, 0, there, s_back, r_back).wait_send()
 
     @pl.loop(0, count)
     def _(k):
@@ -609,13 +603,36 @@
     for stage in range(stages):
         pair_dy_copy(stage).wait_send()
         pair_hid_copy(stage).wait_send()
+
+    cross_send[...] = combine(1, far_meta).astype(BF)
+    cross.start()
+
+    hot = jnp.max(
+        jnp.where(hot_ref[...] == lax.rem(spot, plane), 1.0, 0.0), axis=1, keepdims=True
+    )
+
+    for stage in range(stages):
+        pair_dy_copy(stage).wait_recv()
+        share_half(stage).wait_recv()
+
+    @pl.loop(0, blocks)
+    def _(h):
+        rows = pl.ds(pl.multiple_of(h * BLOCK, BLOCK), BLOCK)
+        theirs = dot_first(pair_hid[:, rows], pair_dy[...])
+        grad_down_ref[rows, :] = (own[rows, :] + hot * theirs).astype(BF)
+
+    cross.wait_recv()
+    grad_tok_ref[...] = (partial[...] + cross_land[...].astype(F32)).astype(BF)
+
+    cross.wait_send()
+
+    @pl.loop(1, plane)
+    def _(hop):
+        there = lax.rem(here + hop, plane)
+        to_plane(back_send, back_land, 1, there, s_back, r_back).wait_send()
+
+    for stage in range(stages):
         share_half(stage).wait_send()
-
-
-def fold_orders():
-    order = np.arange(16 * CAP).reshape(4, 4, CAP).transpose(1, 0, 2).reshape(-1)
-    unfold = np.eye(16 * CAP, dtype=np.float32)[order]
-    return np.stack([unfold, unfold.T])
 
 
 def on_device(
@@ -637,7 +654,7 @@
             jax.ShapeDtypeStruct((tok, width), BF),
             jax.ShapeDtypeStruct((hid, width), BF),
         ),
-        in_specs=[pl.BlockSpec(memory_space=pl.ANY)] * 10,
+        in_specs=[pl.BlockSpec(memory_space=pltpu.HBM)] * 9,
         out_specs=[pl.BlockSpec(memory_space=pltpu.VMEM)] * 2,
         scratch_shapes=[
             pltpu.VMEM(expert_ids.shape[::-1], jnp.int32),
@@ -645,8 +662,8 @@
             pltpu.VMEM(gate_scale.shape[::-1], F32),
             pltpu.VMEM((tok, width), BF),
             pltpu.VMEM((tok, width), BF),
+            pltpu.VMEM((1, hot_pairs.shape[0]), jnp.int32),
             pltpu.VMEM((2, 16 * CAP, 16 * CAP), BF),
-            pltpu.VMEM((1, hot_pairs.shape[0]), jnp.int32),
             pltpu.VMEM((width, hid), BF),
             pltpu.VMEM((width, hid), BF),
             pltpu.VMEM((hid, width), BF),
@@ -677,7 +694,7 @@
             dma((2,)), dma((2,)), dma, dma, dma((2, plane)), dma((2, plane)),
         ] + flow + [
             dma((2, plane)), dma((2, plane)), dma, dma, dma((4,)), dma((4,)),
-            dma((4,)), dma((4,)), dma((4,)), dma((4,)), dma((10,)),
+            dma((4,)), dma((4,)), dma((4,)), dma((4,)), dma((9,)),
         ],
         compiler_params=pltpu.CompilerParams(
             collective_id=0, has_side_effects=True, vmem_limit_bytes=52 * 1024 * 1024
@@ -688,7 +705,7 @@
         name="layer_backward",
     )(
         tokens, cotangent, gate_scale.T, expert_ids.T, expert_slots.T, hot_pairs.reshape(1, -1),
-        jnp.asarray(fold_orders(), dtype=BF), w_gate[0], w_up[0], w_down[0],
+        w_gate[0], w_up[0], w_down[0],
     )
     return grad_tokens, grad_down[None]
 

time: 138 us -> 136 us (0.986)
    unnamed x16 -> x14, local copies, waits for them, and re-layouts: 5.11 us -> 4.18 us
where the time goes in v5:
time: 136 us
  Pallas kernels  131 us (96%)
  local copies, waits for them, and re-layouts  4.18 us (3%)
    pallas_call x1, Pallas kernels, on_device(): pl.pallas_call(layer_kernel, out_shape=(jax.ShapeDtypeStruct((tok, width)...  131 us
    unnamed x14, local copies, waits for them, and re-layouts  4.18 us

profile of v5, /device:TPU:1, one launch (start us, length us, event | category | flops | bytes accessed | tf_op | source)
XLA Modules:
  0.0 135.8 jit_solution(5697428852718118226)
XLA Ops:
  0.6 0.0 copy-start.3
  0.6 0.0 copy-start.2
  0.7 0.0 copy-start.4
  0.7 0.0 copy-start.5
  0.7 0.6 copy-done.3
  1.3 0.0 copy-done.2
  1.3 0.0 copy-done.4
  1.3 0.0 copy-done.5
  1.3 0.0 copy-start
  1.3 0.9 copy-done
  2.3 0.0 copy-start.1
  2.3 0.9 copy-done.1
  3.2 131.0 %layer_backward.1 = (bf16[192,512]{1,0:T(8,128)(2,1)S(1)}, bf16[1024,512]{1,0:T(8,128)(2,1)S(1)}) custom-call(bf16[192,512]{1,0:T(8,128)(2,1)S(1)} %copy-done, bf16[192,512]{1,0:T(8,128)(2,1)S(1)} %copy-done.1, f32[2,192]{1,0:T(2,128)S(1)} %bitcast.9, s32[2,192]{1,0:T(2,128)S(1)} %bitcast.10, s32[2,48]{1,0:T(2,128)S(1)} %bitcast.11, s32[1,16]{1,0:T(1,128)S(1)} %bitcast.12, ...), custom_call_target="tpu_custom_call" | custom-call | flops 4831838208 | bytes 8388608 | tf_op jit(solution)/shard_map/layer_backward/pallas_call | solution.py:651
  134.2 0.7 copy.13
  134.8 1.0 copy.14
Async XLA Ops:
  0.6 0.7 copy-start.3
  0.6 0.7 copy-start.2
  0.7 0.7 copy-start.4
  0.7 0.7 copy-start.5
  1.3 0.9 copy-start
  2.3 0.9 copy-start.1
